TPU v7x, 512 devices: a whole 4x4x16 slice. The times are simulated.
512 devices in a mesh: ha: 16 (over z_hi, x, core), wa: 32 (over z_lo, y).
Axes of the slice: x: 4, y: 4, z: 16 (z_hi: 2, z_lo: 8; z = z_hi * 8 + z_lo), core: 2. Of those that a mesh axis runs over, the one named last changes fastest.
Arguments:
- queries: bfloat16 [256, 448, 1024], P('ha', 'wa'), may hold values from -6 to 6, as said below
- kv_new: bfloat16 [2, 256, 448, 1024], P(None, 'ha', 'wa'), may hold values from -24 to 24
- kv_past: bfloat16 [2, 2, 256, 448, 1024], P(None, None, 'ha', 'wa'), may hold values from -24 to 24
Outputs:
- attended: bfloat16 [256, 448, 1024], P('ha', 'wa')
Inputs may be any that keep to these rules, and one draw needn't show every extreme that they name: `queries`: query entries.
All inputs are finite; a program needn't handle non-finite values.
Results may differ from a plain program's by a relative error of at most 0.0049.
Values may be sent and summed in bfloat16 or wider, within the bound.
A program may use at most 128 MiB of HBM per device.

v0:
```python
import math

import jax
import jax.numpy as jnp
from jax import lax
from jax.sharding import PartitionSpec as P

HEADS = 8
RADIUS = 4


def extended(block, sides, width):
    for axis, dim in sides:
        count = lax.axis_size(axis)
        forward = [(i, i + 1) for i in range(count - 1)]
        backward = [(target, source) for source, target in forward]
        low = lax.ppermute(
            lax.slice_in_dim(block, block.shape[dim] - width, None, axis=dim), axis, forward
        )
        high = lax.ppermute(lax.slice_in_dim(block, 0, width, axis=dim), axis, backward)
        block = jnp.concatenate([low, block, high], axis=dim)
    return block


def widen_tiles(frames):
    return extended(frames, (("ha", 2), ("wa", 3)), RADIUS)


def key_side(queries, kv_new, kv_past):
    tile_rows, tile_cols, width_all = queries.shape
    head_count = HEADS
    head_size = width_all // head_count
    score_scale = 1.0 / math.sqrt(head_size)
    wide_past = widen_tiles(kv_past)
    wide_new = widen_tiles(kv_new[None])
    widened = jnp.concatenate([wide_past, wide_new], 0)
    frame_count = widened.shape[0]
    padded_cols = tile_cols + 2 * RADIUS
    rows_total = tile_rows * lax.axis_size("ha")
    cols_total = tile_cols * lax.axis_size("wa")
    first_row = lax.axis_index("ha") * tile_rows
    first_col = lax.axis_index("wa") * tile_cols
    group_rows = 1
    for candidate in range(1, tile_rows + 1):
        if tile_rows % candidate == 0 and candidate * tile_cols <= 1024:
            group_rows = candidate
    group_count = tile_rows // group_rows
    span_rows = group_rows + 2 * RADIUS
    query_index = jnp.arange(group_rows * tile_cols, dtype=jnp.int32)
    query_row = query_index // tile_cols
    query_col = query_index % tile_cols
    key_index = jnp.arange(span_rows * padded_cols, dtype=jnp.int32)
    key_row = key_index // padded_cols
    key_col = key_index % padded_cols
    row_gap = key_row[None, :] - query_row[:, None]
    col_gap = key_col[None, :] - query_col[:, None]
    near = (row_gap >= 0) & (row_gap <= 2 * RADIUS) & (col_gap >= 0) & (col_gap <= 2 * RADIUS)
    global_col = first_col + key_col - RADIUS
    col_inside = (global_col >= 0) & (global_col < cols_total)

    def one_group(group_index):
        row_start = group_index * group_rows
        key_rows = widened[:, 0].reshape(
            frame_count * span_rows * padded_cols, head_count, head_size
        )
        value_rows = widened[:, 1].reshape(
            frame_count * span_rows * padded_cols, head_count, head_size
        )
        query_block = queries
        query_block = query_block.reshape(group_rows * tile_cols, head_count, head_size)
        scores = (
            jnp.einsum("qhd,khd->hqk", query_block, key_rows, preferred_element_type=jnp.float32)
            * score_scale
        )
        global_row = first_row + row_start + key_row - RADIUS
        row_inside = (global_row >= 0) & (global_row < rows_total)
        allowed = near & (row_inside & col_inside)[None, :]
        allowed = jnp.tile(allowed, (1, frame_count))
        scores = jnp.where(allowed[None], scores, -1e30)
        row_max = jnp.max(scores, -1, keepdims=True)
        weights_raw = jnp.exp(scores - row_max)
        probs = (weights_raw / jnp.sum(weights_raw, -1, keepdims=True)).astype(jnp.bfloat16)
        mixed_out = jnp.einsum(
            "hqk,khd->qhd", probs, value_rows, preferred_element_type=jnp.float32
        )
        return mixed_out.reshape(group_rows, tile_cols, width_all).astype(jnp.bfloat16)

    results = lax.map(one_group, jnp.arange(group_count, dtype=jnp.int32))
    return results.reshape(tile_rows, tile_cols, width_all)


def on_device(queries, kv_new, kv_past):
    return key_side(queries, kv_new, kv_past)


def solution(mesh):
    return jax.shard_map(
        on_device,
        mesh=mesh,
        in_specs=(P("ha", "wa", None), P(None, "ha", "wa", None), P(None, None, "ha", "wa", None)),
        out_specs=P("ha", "wa", None),
        check_vma=False,
    )
```

profile of v0, /device:TPU:480, one launch (start us, length us, event | category | flops | bytes accessed | tf_op | source)
XLA Modules:
  0.0 147.2 jit_solution(2058378466184542972)
XLA Ops:
  0.0 2.0 %fusion.32 = (bf16[2,2,4,14,1024]{4,2,3,1,0:T(4,128)(2,1)S(1)}, bf16[2,2,4,14,1024]{4,2,3,1,0:T(4,128)(2,1)S(1)}) fusion(bf16[2,2,16,14,1024]{4,2,3,1,0:T(8,128)(2,1)} %param.5), kind=kLoop, calls=%fused_computation.54 | loop fusion | bytes 1835008 | tf_op jit(solution)/shard_map/slice | solution.py:18
  2.2 8.0 %collective-permute-start.1 = (bf16[2,2,4,14,1024]{4,3,2,1,0:T(8,128)(2,1)S(1)}, bf16[2,2,4,14,1024]{4,3,2,1,0:T(8,128)(2,1)S(1)}, u32[]{:S(2)}, u32[]{:S(2)}) collective-permute-start(bf16[2,2,4,14,1024]{4,3,2,1,0:T(8,128)(2,1)S(1)} %copy.27), channel_id=1, source_target_pairs={{32,0},{64,32},{96,64},{128,96},{160,128},{192,160},{224,192},{256... | collective-permute-start | bytes 1376264 | tf_op jit(solution)/shard_map/ppermute | solution.py:20
  10.3 1.9 %collective-permute-start = (bf16[2,2,4,14,1024]{4,3,2,1,0:T(8,128)(2,1)S(1)}, bf16[2,2,4,14,1024]{4,3,2,1,0:T(8,128)(2,1)S(1)}, u32[]{:S(2)}, u32[]{:S(2)}) collective-permute-start(bf16[2,2,4,14,1024]{4,3,2,1,0:T(8,128)(2,1)S(1)} %copy.26), channel_id=1, source_target_pairs={{0,32},{32,64},{64,96},{96,128},{128,160},{160,192},{192,224},{224... | collective-permute-start | bytes 1376264 | tf_op jit(solution)/shard_map/ppermute | solution.py:17
  12.2 2.1 %fusion.33 = (bf16[1,2,4,14,1024]{4,2,3,1,0:T(4,128)(2,1)}, bf16[1,2,4,14,1024]{4,2,3,1,0:T(4,128)(2,1)}) fusion(bf16[1,2,16,14,1024]{4,2,3,1,0:T(8,128)(2,1)} %bitcast.19), kind=kLoop, calls=%fused_computation.55 | loop fusion | bytes 917504 | tf_op jit(solution)/shard_map/slice | solution.py:18
  14.4 1.9 %collective-permute-start.4 = (bf16[1,2,4,14,1024]{4,2,3,1,0:T(4,128)(2,1)}, bf16[1,2,4,14,1024]{4,2,3,1,0:T(4,128)(2,1)S(1)}, u32[]{:S(2)}, u32[]{:S(2)}) collective-permute-start(bf16[1,2,4,14,1024]{4,2,3,1,0:T(4,128)(2,1)} %get-tuple-element.37), channel_id=1, source_target_pairs={{0,32},{32,64},{64,96},{96,128},{128,160},{160,192},{192,224},{224... | collective-permute-start | bytes 688136 | tf_op jit(solution)/shard_map/ppermute | solution.py:17
  16.3 14.5 %collective-permute-start.5 = (bf16[1,2,4,14,1024]{4,2,3,1,0:T(4,128)(2,1)}, bf16[1,2,4,14,1024]{4,2,3,1,0:T(4,128)(2,1)}, u32[]{:S(2)}, u32[]{:S(2)}) collective-permute-start(bf16[1,2,4,14,1024]{4,2,3,1,0:T(4,128)(2,1)} %get-tuple-element.38), channel_id=1, source_target_pairs={{32,0},{64,32},{96,64},{128,96},{160,128},{192,160},{224,192},{256... | collective-permute-start | bytes 688136 | tf_op jit(solution)/shard_map/ppermute | solution.py:20
  30.8 0.4 copy.16
  31.1 0.8 collective-permute-done
  31.9 0.4 copy.15
  32.3 0.8 copy-done.2
  33.1 2.0 %pad_maximum_fusion.2 = (bf16[2,2,24,4,1024]{4,2,3,1,0:T(8,128)(2,1)}, bf16[2,2,24,4,1024]{4,2,3,1,0:T(8,128)(2,1)}) fusion(bf16[2,2,4,14,1024]{4,2,3,1,0:T(4,128)(2,1)S(1)} %copy.16, bf16[2,2,16,14,1024]{4,2,3,1,0:T(8,128)(2,1)S(1)} %copy-done, bf16[2,2,4,14,1024]{4,2,3,1,0:T(4,128)(2,1)S(1)} %copy.15), kind=kLoop, calls=%fused_computation.17 | loop fusion | flops 4718592 | bytes 4325376 | tf_op jit(solution)/shard_map/slice | solution.py:18
  35.0 3.5 %collective-permute-start.2 = (bf16[2,2,24,4,1024]{4,2,3,1,0:T(8,128)(2,1)}, bf16[2,2,24,4,1024]{4,2,3,1,0:T(8,128)(2,1)}, u32[]{:S(2)}, u32[]{:S(2)}) collective-permute-start(bf16[2,2,24,4,1024]{4,2,3,1,0:T(8,128)(2,1)} %get-tuple-element.21), channel_id=1, source_target_pairs={{0,1},{1,2},{2,3},{3,4},{4,5},{5,6},{6,7},{7,8},{8,9},{9,10},{10,1... | collective-permute-start | bytes 2359304 | tf_op jit(solution)/shard_map/ppermute | solution.py:17
  38.5 30.4 %collective-permute-start.3 = (bf16[2,2,24,4,1024]{4,2,3,1,0:T(8,128)(2,1)}, bf16[2,2,24,4,1024]{4,2,3,1,0:T(8,128)(2,1)}, u32[]{:S(2)}, u32[]{:S(2)}) collective-permute-start(bf16[2,2,24,4,1024]{4,2,3,1,0:T(8,128)(2,1)} %get-tuple-element.22), channel_id=1, source_target_pairs={{1,0},{2,1},{3,2},{4,3},{5,4},{6,5},{7,6},{8,7},{9,8},{10,9},{11,1... | collective-permute-start | bytes 2359304 | tf_op jit(solution)/shard_map/ppermute | solution.py:20
  69.0 2.2 %pad_maximum_fusion.5 = (bf16[1,2,24,4,1024]{4,2,3,1,0:T(8,128)(2,1)}, bf16[1,2,24,4,1024]{4,2,3,1,0:T(8,128)(2,1)}) fusion(bf16[1,2,4,14,1024]{4,2,3,1,0:T(4,128)(2,1)} %collective-permute-done.5, bf16[1,2,16,14,1024]{4,2,3,1,0:T(8,128)(2,1)S(1)} %bitcast.20, bf16[1,2,4,14,1024]{4,2,3,1,0:T(4,128)(2,1)S(1)} %collective-permute-done.4), kind=kLoop, calls=%fused_computation.29 | loop fusion | flops 2359296 | bytes 2162688 | tf_op jit(solution)/shard_map/slice | solution.py:18
  71.2 1.9 %collective-permute-start.6 = (bf16[1,2,24,4,1024]{4,2,3,1,0:T(8,128)(2,1)}, bf16[1,2,24,4,1024]{4,2,3,1,0:T(8,128)(2,1)}, u32[]{:S(2)}, u32[]{:S(2)}) collective-permute-start(bf16[1,2,24,4,1024]{4,2,3,1,0:T(8,128)(2,1)} %get-tuple-element.34), channel_id=1, source_target_pairs={{0,1},{1,2},{2,3},{3,4},{4,5},{5,6},{6,7},{7,8},{8,9},{9,10},{10,1... | collective-permute-start | bytes 1179656 | tf_op jit(solution)/shard_map/ppermute | solution.py:17
  73.1 6.0 %collective-permute-start.7 = (bf16[1,2,24,4,1024]{4,2,3,1,0:T(8,128)(2,1)}, bf16[1,2,24,4,1024]{4,2,3,1,0:T(8,128)(2,1)}, u32[]{:S(2)}, u32[]{:S(2)}) collective-permute-start(bf16[1,2,24,4,1024]{4,2,3,1,0:T(8,128)(2,1)} %get-tuple-element.36), channel_id=1, source_target_pairs={{1,0},{2,1},{3,2},{4,3},{5,4},{6,5},{7,6},{8,7},{9,8},{10,9},{11,1... | collective-permute-start | bytes 1179656 | tf_op jit(solution)/shard_map/ppermute | solution.py:20
  79.2 0.3 fusion.18
  79.5 0.9 tile.14
  80.3 2.2 %copy.18 = pred[224,1584]{1,0:T(8,128)(4,1)} copy(pred[224,1584]{0,1:T(8,128)(4,1)} %bitcast.22) | data formatting | bytes 709632 | tf_op jit(solution)/shard_map/while/body/eval_jaxpr/tile | solution.py:78
  82.6 2.1 %copy.20 = bf16[16,14,1024]{2,1,0:T(8,128)(2,1)} copy(bf16[16,14,1024]{2,0,1:T(8,128)(2,1)} %param.3) | data formatting | bytes 917504 | tf_op args[0]
  84.7 2.2 %reshape.142 = bf16[224,8,128]{2,1,0:T(8,128)(2,1)} reshape(bf16[16,14,1024]{2,1,0:T(8,128)(2,1)} %copy.20) | data formatting | bytes 917504 | tf_op jit(solution)/shard_map/while/body/eval_jaxpr/reshape | solution.py:70
  86.9 4.8 %maximum_maximum_fusion = bf16[3,2,24,22,1024]{4,2,3,1,0:T(8,128)(2,1)S(1)} fusion(bf16[1,2,24,4,1024]{4,2,3,1,0:T(8,128)(2,1)} %collective-permute-done.7, bf16[1,2,4,14,1024]{4,2,3,1,0:T(4,128)(2,1)} %collective-permute-done.5, bf16[1,2,16,14,1024]{4,2,3,1,0:T(8,128)(2,1)S(1)} %bitcast.21, bf16[1,2,4,14,1024]{4,2,3,1,0:T(4,128)(2,1)S(1)} %collective-permute-done.4, ...), kind=kLoop, calls=%fused_computation.5 | loop fusion | flops 64880640 | bytes 12976128 | tf_op jit(solution)/shard_map/concatenate | solution.py:36
  91.7 2.6 %fusion.31 = (bf16[3,1,24,22,1024]{4,2,3,1,0:T(8,128)(2,1)S(1)}, bf16[3,1,24,22,1024]{4,2,3,1,0:T(8,128)(2,1)}) fusion(bf16[3,2,24,22,1024]{4,2,3,1,0:T(8,128)(2,1)S(1)} %maximum_maximum_fusion), kind=kLoop, calls=%fused_computation.53 | loop fusion | bytes 12976128 | tf_op jit(solution)/shard_map/while/body/eval_jaxpr/slice | solution.py:63
  94.2 3.6 %copy.19 = bf16[3,1,24,22,1024]{4,3,2,0,1:T(8,128)(2,1)} copy(bf16[3,1,24,22,1024]{4,2,3,1,0:T(8,128)(2,1)S(1)} %get-tuple-element.19) | data formatting | bytes 6488064 | tf_op jit(solution)/shard_map/while/body/eval_jaxpr/slice | solution.py:63
  97.8 4.7 %squeeze.12 = bf16[1584,8,128]{2,1,0:T(8,128)(2,1)S(1)} reshape(bf16[3,1,24,22,1024]{4,3,2,0,1:T(8,128)(2,1)} %copy.19) | data formatting | bytes 6488064 | tf_op jit(solution)/shard_map/while/body/eval_jaxpr/reshape;while/body/eval_jaxpr/squeeze | solution.py:63
  102.5 5.5 %copy.17 = bf16[3,1,24,22,1024]{4,3,2,0,1:T(8,128)(2,1)} copy(bf16[3,1,24,22,1024]{4,2,3,1,0:T(8,128)(2,1)} %get-tuple-element.20) | data formatting | bytes 6488064 | tf_op jit(solution)/shard_map/while/body/eval_jaxpr/slice | solution.py:66
  108.0 6.1 %squeeze.11 = bf16[1584,8,128]{2,1,0:T(8,128)(2,1)} reshape(bf16[3,1,24,22,1024]{4,3,2,0,1:T(8,128)(2,1)} %copy.17) | data formatting | bytes 6488064 | tf_op jit(solution)/shard_map/while/body/eval_jaxpr/reshape;while/body/eval_jaxpr/squeeze | solution.py:66
  114.1 7.2 %fusion.7 = f32[8,1584,224]{1,2,0:T(8,128)} fusion(bf16[1584,8,128]{2,1,0:T(8,128)(2,1)S(1)} %squeeze.12, bf16[224,8,128]{2,1,0:T(8,128)(2,1)} %reshape.142), kind=kOutput, calls=%fused_computation.11 | convolution fusion | flops 726663168 | bytes 15056896 | tf_op jit(solution)/shard_map/while/body/eval_jaxpr/qhd,khd->hqk/dot_general | solution.py:72
  121.3 17.9 %fusion.34 = (f32[8,224]{1,0:T(8,128)S(1)}, f32[8,224,1584]{2,1,0:T(8,128)}) fusion(f32[8,1584,224]{1,2,0:T(8,128)} %fusion.7, pred[224,1584]{1,0:T(8,128)(4,1)} %copy.18), kind=kOutput, calls=%fused_computation.56 | output fusion | flops 17032752 | bytes 23070208 | tf_op jit(solution)/shard_map/while/body/eval_jaxpr/sub | solution.py:81
  139.2 6.4 %fusion.12 = bf16[224,8,128]{2,0,1:T(8,128)(2,1)S(1)} fusion(bf16[1584,8,128]{2,1,0:T(8,128)(2,1)S(1)} %copy-done.3, f32[8,224,1584]{2,1,0:T(8,128)} %get-tuple-element.40, f32[8,224]{1,0:T(8,128)S(1)} %get-tuple-element.39), kind=kOutput, calls=%fused_computation.14 | convolution fusion | flops 732569600 | bytes 15064064 | tf_op jit(solution)/shard_map/while/body/eval_jaxpr/hqk,khd->qhd/dot_general | solution.py:83
  145.8 0.4 convert_element_type.18
  146.2 1.0 copy.25
  (20 shorter events, 0.6 us)
Async XLA Ops:
  0.0 33.1 %copy-start = (bf16[2,2,16,14,1024]{4,2,3,1,0:T(8,128)(2,1)S(1)}, bf16[2,2,16,14,1024]{4,2,3,1,0:T(8,128)(2,1)}, u32[]{:S(2)}) copy-start(bf16[2,2,16,14,1024]{4,2,3,1,0:T(8,128)(2,1)} %param.5) | copy-start | bytes 5505028
  0.0 69.0 %copy-start.1 = (bf16[2,16,14,1024]{3,1,2,0:T(8,128)(2,1)S(1)}, bf16[2,16,14,1024]{3,1,2,0:T(8,128)(2,1)}, u32[]{:S(2)}) copy-start(bf16[2,16,14,1024]{3,1,2,0:T(8,128)(2,1)} %param.4) | copy-start | bytes 2752516
  2.2 28.6 %collective-permute-start.1 = (bf16[2,2,4,14,1024]{4,3,2,1,0:T(8,128)(2,1)S(1)}, bf16[2,2,4,14,1024]{4,3,2,1,0:T(8,128)(2,1)S(1)}, u32[]{:S(2)}, u32[]{:S(2)}) collective-permute-start(bf16[2,2,4,14,1024]{4,3,2,1,0:T(8,128)(2,1)S(1)} %copy.27), channel_id=1, source_target_pairs={{32,0},{64,32},{96,64},{128,96},{160,128},{192,160},{224,192},{256... | collective-permute-start | bytes 1376264 | tf_op jit(solution)/shard_map/ppermute | solution.py:20
  10.3 21.6 %collective-permute-start = (bf16[2,2,4,14,1024]{4,3,2,1,0:T(8,128)(2,1)S(1)}, bf16[2,2,4,14,1024]{4,3,2,1,0:T(8,128)(2,1)S(1)}, u32[]{:S(2)}, u32[]{:S(2)}) collective-permute-start(bf16[2,2,4,14,1024]{4,3,2,1,0:T(8,128)(2,1)S(1)} %copy.26), channel_id=1, source_target_pairs={{0,32},{32,64},{64,96},{96,128},{128,160},{160,192},{192,224},{224... | collective-permute-start | bytes 1376264 | tf_op jit(solution)/shard_map/ppermute | solution.py:17
  14.4 54.6 %collective-permute-start.4 = (bf16[1,2,4,14,1024]{4,2,3,1,0:T(4,128)(2,1)}, bf16[1,2,4,14,1024]{4,2,3,1,0:T(4,128)(2,1)S(1)}, u32[]{:S(2)}, u32[]{:S(2)}) collective-permute-start(bf16[1,2,4,14,1024]{4,2,3,1,0:T(4,128)(2,1)} %get-tuple-element.37), channel_id=1, source_target_pairs={{0,32},{32,64},{64,96},{96,128},{128,160},{160,192},{192,224},{224... | collective-permute-start | bytes 688136 | tf_op jit(solution)/shard_map/ppermute | solution.py:17
  16.3 52.7 %collective-permute-start.5 = (bf16[1,2,4,14,1024]{4,2,3,1,0:T(4,128)(2,1)}, bf16[1,2,4,14,1024]{4,2,3,1,0:T(4,128)(2,1)}, u32[]{:S(2)}, u32[]{:S(2)}) collective-permute-start(bf16[1,2,4,14,1024]{4,2,3,1,0:T(4,128)(2,1)} %get-tuple-element.38), channel_id=1, source_target_pairs={{32,0},{64,32},{96,64},{128,96},{160,128},{192,160},{224,192},{256... | collective-permute-start | bytes 688136 | tf_op jit(solution)/shard_map/ppermute | solution.py:20
  32.3 0.8 copy-start.2
  35.0 51.8 %collective-permute-start.2 = (bf16[2,2,24,4,1024]{4,2,3,1,0:T(8,128)(2,1)}, bf16[2,2,24,4,1024]{4,2,3,1,0:T(8,128)(2,1)}, u32[]{:S(2)}, u32[]{:S(2)}) collective-permute-start(bf16[2,2,24,4,1024]{4,2,3,1,0:T(8,128)(2,1)} %get-tuple-element.21), channel_id=1, source_target_pairs={{0,1},{1,2},{2,3},{3,4},{4,5},{5,6},{6,7},{7,8},{8,9},{9,10},{10,1... | collective-permute-start | bytes 2359304 | tf_op jit(solution)/shard_map/ppermute | solution.py:17
  38.5 48.3 %collective-permute-start.3 = (bf16[2,2,24,4,1024]{4,2,3,1,0:T(8,128)(2,1)}, bf16[2,2,24,4,1024]{4,2,3,1,0:T(8,128)(2,1)}, u32[]{:S(2)}, u32[]{:S(2)}) collective-permute-start(bf16[2,2,24,4,1024]{4,2,3,1,0:T(8,128)(2,1)} %get-tuple-element.22), channel_id=1, source_target_pairs={{1,0},{2,1},{3,2},{4,3},{5,4},{6,5},{7,6},{8,7},{9,8},{10,9},{11,1... | collective-permute-start | bytes 2359304 | tf_op jit(solution)/shard_map/ppermute | solution.py:20
  71.2 15.7 %collective-permute-start.6 = (bf16[1,2,24,4,1024]{4,2,3,1,0:T(8,128)(2,1)}, bf16[1,2,24,4,1024]{4,2,3,1,0:T(8,128)(2,1)}, u32[]{:S(2)}, u32[]{:S(2)}) collective-permute-start(bf16[1,2,24,4,1024]{4,2,3,1,0:T(8,128)(2,1)} %get-tuple-element.34), channel_id=1, source_target_pairs={{0,1},{1,2},{2,3},{3,4},{4,5},{5,6},{6,7},{7,8},{8,9},{9,10},{10,1... | collective-permute-start | bytes 1179656 | tf_op jit(solution)/shard_map/ppermute | solution.py:17
  73.1 13.8 %collective-permute-start.7 = (bf16[1,2,24,4,1024]{4,2,3,1,0:T(8,128)(2,1)}, bf16[1,2,24,4,1024]{4,2,3,1,0:T(8,128)(2,1)}, u32[]{:S(2)}, u32[]{:S(2)}) collective-permute-start(bf16[1,2,24,4,1024]{4,2,3,1,0:T(8,128)(2,1)} %get-tuple-element.36), channel_id=1, source_target_pairs={{1,0},{2,1},{3,2},{4,3},{5,4},{6,5},{7,6},{8,7},{9,8},{10,9},{11,1... | collective-permute-start | bytes 1179656 | tf_op jit(solution)/shard_map/ppermute | solution.py:20
  121.3 17.9 %copy-start.3 = (bf16[1584,8,128]{2,1,0:T(8,128)(2,1)S(1)}, bf16[1584,8,128]{2,1,0:T(8,128)(2,1)}, u32[]{:S(2)}) copy-start(bf16[1584,8,128]{2,1,0:T(8,128)(2,1)} %squeeze.11) | copy-start | bytes 9732100
where the time goes:
time: 148 us; the launch traced here: 147 us
  starting transfers between devices  68.1 us (46%)
  local copies, waits for them, and re-layouts  37.3 us (25%)
  other arithmetic  27.2 us (18%)
  matrix products  13.6 us (9%)
    ppermute x4, starting transfers between devices, extended(): lax.ppermute(lax.slice_in_dim(block, 0, width, axis=dim), axis, backward)  58.9 us
    sub x1, other arithmetic, one_group(): weights_raw = jnp.exp(scores - row_max)  17.9 us
    ppermute x4, starting transfers between devices, extended(): lax.ppermute(lax.slice_in_dim(block, block.shape[dim] - width, None, axis...  9.21 us
    dot_general x1, matrix products, one_group(): jnp.einsum('qhd,khd->hqk', query_block, key_rows, preferred_element_type=...  7.18 us
    dot_general x1, matrix products, one_group(): jnp.einsum('hqk,khd->qhd', probs, value_rows, preferred_element_type=jnp....  6.4 us
    squeeze x1, local copies, waits for them, and re-layouts, one_group(): widened[:, 1]  6.14 us
    slice x2, local copies, waits for them, and re-layouts, one_group(): widened[:, 0]  6.11 us
    slice x1, local copies, waits for them, and re-layouts, one_group(): widened[:, 1]  5.47 us
  transfers between devices with their start and end apart: 8, of which 1 were waited for; matrix products, arithmetic and copies ran while one was open for 10% of the time, Pallas kernels for 0%

commit v1 on v0

v1 whole, which is shorter than its diff:
```python
import functools
import math

import jax
import jax.numpy as jnp
from jax import lax
from jax.experimental import pallas as pl
from jax.experimental.pallas import tpu as pltpu
from jax.sharding import PartitionSpec as P

MESH = pl.DeviceIdType.MESH
HEADS = 8
DIM = 128
RADIUS = 4
FRAMES = 3
ROWS = 16
COLS = 14
PAD = 16
TOKENS = ROWS * PAD
SIDE = ROWS * RADIUS
EDGE = RADIUS * PAD
CORNER = RADIUS * RADIUS
CHUNKS = 4
LOW = -1e30
FOLD = math.log2(math.e) / math.sqrt(DIM)
F32 = jnp.float32
BF16 = jnp.bfloat16


def dot_nt(a, b):
    return lax.dot_general(a, b, (((1,), (1,)), ((), ())), preferred_element_type=F32)


def dot_nn(a, b, precision=None):
    return lax.dot_general(
        a, b, (((1,), (0,)), ((), ())), preferred_element_type=F32, precision=precision
    )


def iota(shape, dim):
    return lax.broadcasted_iota(jnp.int32, shape, dim)


def lanes(head):
    return pl.ds(pl.multiple_of(head * DIM, DIM), DIM)


def kernel(
    nh, nw,
    q_hbm, new_hbm, past_hbm, out_hbm,
    q_in, kv_in, out_v, q_all, kv_all, q_side, kv_side,
    q_edge, q_flank, ext, own_o, own_m, own_l,
    send_o, send_s, edge_o, edge_s, flank_o, flank_s,
    bias_own, bias_flank, bias_edge, pick, side_stat,
    load_sem, store_sem,
    q_edge_sem, q_flank_sem, ext_sem, edge_sem, flank_sem, stat_sem,
):
    h = lax.axis_index("ha")
    w = lax.axis_index("wa")
    has_up, has_down = h > 0, h < nh - 1
    has_left, has_right = w > 0, w < nw - 1
    up, down = (h - 1, w), (h + 1, w)
    left, right = (h, w - 1), (h, w + 1)
    flip = (h == nh // 2).astype(jnp.int32)

    barrier = pltpu.get_barrier_semaphore()
    for there, device in ((has_up, up), (has_down, down), (has_left, left), (has_right, right)):
        @pl.when(there)
        def _():
            pl.semaphore_signal(barrier, inc=1, device_id=device, device_id_type=MESH)

    loads = [pltpu.make_async_copy(q_hbm, q_in, load_sem.at[0])]
    for kv in range(2):
        for f in range(FRAMES):
            source = new_hbm.at[kv] if f == FRAMES - 1 else past_hbm.at[f, kv]
            slot = kv * FRAMES + f
            loads.append(pltpu.make_async_copy(source, kv_in.at[slot], load_sem.at[1 + slot]))
    for load in loads:
        load.start()

    qi, ki = iota((TOKENS, TOKENS), 0), iota((TOKENS, TOKENS), 1)
    near = (
        (abs(qi // PAD - ki // PAD) <= RADIUS)
        & (abs(qi % PAD - ki % PAD) <= RADIUS)
        & (ki % PAD < COLS)
    )
    bias_own[...] = jnp.where(near, 0.0, LOW)

    qi, ki = iota((SIDE, FRAMES * SIDE), 0), iota((SIDE, FRAMES * SIDE), 1) % SIDE
    rows_near = abs(qi // RADIUS - ki // RADIUS) <= RADIUS
    bias_flank[0] = jnp.where(rows_near & (ki % RADIUS <= qi % RADIUS), 0.0, LOW)
    bias_flank[1] = jnp.where(rows_near & (ki % RADIUS >= qi % RADIUS), 0.0, LOW)

    span = EDGE + 2 * CORNER
    qi, ki = iota((EDGE, FRAMES * span), 0), iota((EDGE, FRAMES * span), 1) % span
    in_left = (ki >= EDGE) & (ki < EDGE + CORNER)
    in_right = ki >= EDGE + CORNER
    corner = (ki - EDGE) % CORNER
    key_row = jnp.where(ki < EDGE, ki // PAD, corner // RADIUS)
    key_col = jnp.where(
        ki < EDGE,
        ki % PAD,
        jnp.where(in_left, corner % RADIUS - RADIUS, corner % RADIUS + COLS),
    )
    real = jnp.where(
        in_left,
        has_left.astype(jnp.int32),
        jnp.where(in_right, has_right.astype(jnp.int32), (ki % PAD < COLS).astype(jnp.int32)),
    )
    cols_near = (abs(qi % PAD - key_col) <= RADIUS) & (real > 0)
    bias_edge[0] = jnp.where(cols_near & (key_row <= qi // PAD), 0.0, LOW)
    bias_edge[1] = jnp.where(cols_near & (key_row >= qi // PAD), 0.0, LOW)

    pi, pt = iota((2 * SIDE, TOKENS), 0), iota((2 * SIDE, TOKENS), 1)
    pl_token = pi % SIDE // RADIUS * PAD + pi % RADIUS + jnp.where(pi < SIDE, 0, COLS - RADIUS)
    pick[...] = jnp.where(pt == pl_token, 1.0, 0.0).astype(BF16)

    q_all[...] = jnp.zeros_like(q_all)
    for slot in range(2 * FRAMES):
        kv_all[slot] = jnp.zeros_like(kv_all[slot])

    loads[0].wait()
    for r in range(ROWS):
        q_all[r * PAD : r * PAD + COLS, :] = q_in[r]
    q_side[...] = dot_nn(pick[...], q_all[...]).astype(BF16)

    for there, side in ((has_up, 0), (has_down, 1)):
        @pl.when(jnp.logical_not(there))
        def _():
            edge_o[side] = jnp.zeros_like(edge_o[side])
            edge_s[side] = jnp.full(edge_s.shape[1:], LOW, F32)
    for there, side in ((has_left, 0), (has_right, 1)):
        @pl.when(jnp.logical_not(there))
        def _():
            flank_o[side * SIDE : (side + 1) * SIDE, :] = jnp.zeros((SIDE, HEADS * DIM), BF16)
            flank_s[side] = jnp.full(flank_s.shape[1:], LOW, F32)
            for s in range(2):
                ext[s, :, side * CORNER : (side + 1) * CORNER, :] = jnp.zeros(
                    (2 * FRAMES, CORNER, HEADS * DIM), BF16
                )

    def remote(src, dst, sems, index, device):
        return pltpu.make_async_remote_copy(
            src_ref=src,
            dst_ref=dst,
            send_sem=sems.at[(0, *index)],
            recv_sem=sems.at[(1, *index)],
            device_id=device,
            device_id_type=MESH,
        )

    width = HEADS * DIM // CHUNKS

    def copy_q_edge(side, c, device):
        part = pl.ds(c * width, width)
        first = (1 - side) * (TOKENS - EDGE)
        return remote(
            q_all.at[pl.ds(first, EDGE), part],
            q_edge.at[side, :, part],
            q_edge_sem,
            (side, c),
            device,
        )

    def copy_q_flank(side, device):
        return remote(
            q_side.at[pl.ds((1 - side) * SIDE, SIDE)],
            q_flank.at[side],
            q_flank_sem,
            (side,),
            device,
        )

    def copy_ext(side, s, device):
        return remote(
            kv_side.at[:, pl.ds((1 - side) * SIDE + s * (SIDE - CORNER), CORNER)],
            ext.at[s, :, pl.ds(side * CORNER, CORNER)],
            ext_sem,
            (side, s),
            device,
        )

    def copy_edge_o(side, c, device):
        part = pl.ds(c * width, width)
        return remote(
            send_o.at[side, :, part],
            edge_o.at[1 - side, :, part],
            edge_sem,
            (1 - side, c),
            device,
        )

    def copy_edge_s(side, device):
        return remote(send_s.at[side], edge_s.at[1 - side], stat_sem, (1 - side,), device)

    def copy_flank_o(side, device):
        return remote(
            send_o.at[2 + side],
            flank_o.at[pl.ds((1 - side) * SIDE, SIDE)],
            flank_sem,
            (1 - side,),
            device,
        )

    def copy_flank_s(side, device):
        return remote(send_s.at[2 + side], flank_s.at[1 - side], stat_sem, (3 - side,), device)

    n_near = (
        has_up.astype(jnp.int32)
        + has_down.astype(jnp.int32)
        + has_left.astype(jnp.int32)
        + has_right.astype(jnp.int32)
    )
    pl.semaphore_wait(barrier, n_near)

    for c in range(CHUNKS):
        @pl.when(has_down)
        def _():
            copy_q_edge(0, c, down).start()

        @pl.when(has_up)
        def _():
            copy_q_edge(1, c, up).start()

    @pl.when(has_right)
    def _():
        copy_q_flank(0, right).start()

    @pl.when(has_left)
    def _():
        copy_q_flank(1, left).start()

    for slot in range(2 * FRAMES):
        loads[1 + slot].wait()
        for r in range(ROWS):
            kv_all[slot, r * PAD : r * PAD + COLS, :] = kv_in[slot, r]
        kv_side[slot] = dot_nn(pick[...], kv_all[slot]).astype(BF16)

    for s in range(2):
        @pl.when(has_right)
        def _():
            copy_ext(0, s, right).start()

        @pl.when(has_left)
        def _():
            copy_ext(1, s, left).start()

    def soft(scores, top):
        return jnp.exp2(scores * FOLD - top).astype(BF16)

    def with_ones(values):
        return jnp.concatenate([values, jnp.ones_like(values)], axis=1)

    half = TOKENS // 2
    cut = TOKENS - EDGE

    def own_head(head, carry):
        at = lanes(head)
        q = q_all[:, at]
        k0, k1 = [
            jnp.concatenate([kv_all[f, pl.ds(b * half, half), at] for f in range(FRAMES)], axis=0)
            for b in range(2)
        ]
        v0, v1 = [
            jnp.concatenate(
                [kv_all[FRAMES + f, pl.ds(b * half, half), at] for f in range(FRAMES)], axis=0
            )
            for b in range(2)
        ]
        b0 = bias_own[0:cut, 0:half]
        b1 = bias_own[EDGE:TOKENS, half:TOKENS]
        s0 = dot_nt(q[0:cut], k0) + jnp.concatenate([b0] * FRAMES, axis=1)
        s1 = dot_nt(q[EDGE:TOKENS], k1) + jnp.concatenate([b1] * FRAMES, axis=1)
        t0 = jnp.max(s0, axis=1, keepdims=True)
        t1 = jnp.max(s1, axis=1, keepdims=True)
        top = FOLD * jnp.concatenate(
            [t0[0:EDGE], jnp.maximum(t0[EDGE:cut], t1[0 : cut - EDGE]), t1[cut - EDGE :]], axis=0
        )
        o0 = dot_nn(soft(s0, top[0:cut]), with_ones(v0))
        o1 = dot_nn(soft(s1, top[EDGE:TOKENS]), with_ones(v1))
        both = jnp.concatenate(
            [o0[0:EDGE], o0[EDGE:cut] + o1[0 : cut - EDGE], o1[cut - EDGE :]], axis=0
        )
        own_o[head] = both[:, :DIM]
        own_l[head] = both[:, DIM:]
        own_m[head] = jnp.broadcast_to(top, (TOKENS, DIM))
        return carry

    lax.fori_loop(0, HEADS, own_head, 0)

    lane = iota((PAD, DIM), 1)

    def guest_head(head, stat, q, k, v, bias):
        s = dot_nt(q, k) + bias
        top = FOLD * jnp.max(s, axis=1, keepdims=True)
        both = dot_nn(soft(s, top), with_ones(v))
        for t in range(RADIUS):
            group = slice(t * PAD, (t + 1) * PAD)
            stat = jnp.where(lane == 32 * t + head, top[group], stat)
            stat = jnp.where(lane == 32 * t + HEADS + head, both[group, DIM:], stat)
        return both[:, :DIM].astype(BF16), stat

    for side, there, device in ((0, has_left, left), (1, has_right, right)):
        @pl.when(there)
        def _():
            copy_q_flank(side, device).wait_recv()

            def flank_head(head, stat):
                at = lanes(head)
                part = pl.ds(side * SIDE, SIDE)
                k = jnp.concatenate([kv_side[f, part, at] for f in range(FRAMES)], axis=0)
                v = jnp.concatenate([kv_side[FRAMES + f, part, at] for f in range(FRAMES)], axis=0)
                o, stat = guest_head(head, stat, q_flank[side, :, at], k, v, bias_flank[side])
                send_o[2 + side, :, at] = o
                return stat

            send_s[2 + side] = lax.fori_loop(0, HEADS, flank_head, jnp.zeros((PAD, DIM), F32))
            copy_flank_o(side, device).start()
            copy_flank_s(side, device).start()

    for side, there, device in ((0, has_left, left), (1, has_right, right)):
        @pl.when(there)
        def _():
            for s in range(2):
                copy_ext(side, s, device).wait_recv()

    per = HEADS // CHUNKS
    for turn in range(2):
        side = (turn + flip) % 2
        there = jnp.where(side == 0, has_up.astype(jnp.int32), has_down.astype(jnp.int32)) > 0
        device = (h - 1 + 2 * side, w)

        @pl.when(there)
        def _():
            def edge_chunk(c, stat):
                copy_q_edge(side, c, device).wait_recv()

                def edge_head(i, stat):
                    head = c * per + i
                    at = lanes(head)
                    part = pl.ds(pl.multiple_of(side * (TOKENS - EDGE), EDGE), EDGE)

                    def keys(kv):
                        pieces = []
                        for f in range(FRAMES):
                            pieces.append(kv_all[kv * FRAMES + f, part, at])
                            pieces.append(ext[side, kv * FRAMES + f, :, at])
                        return jnp.concatenate(pieces, axis=0)

                    o, stat = guest_head(
                        head, stat, q_edge[side, :, at], keys(0), keys(1), bias_edge[side]
                    )
                    send_o[side, :, at] = o
                    return stat

                for i in range(per):
                    stat = edge_head(i, stat)
                copy_edge_o(side, c, device).start()
                return stat

            stat = jnp.zeros((PAD, DIM), F32)
            for c in range(CHUNKS):
                stat = edge_chunk(c, stat)
            send_s[side] = stat
            copy_edge_s(side, device).start()

    for side, there, device in ((0, has_left, left), (1, has_right, right)):
        @pl.when(there)
        def _():
            copy_flank_o(1 - side, device).wait_recv()
            copy_flank_s(1 - side, device).wait_recv()

    packed = []
    for side in range(2):
        for t in range(RADIUS):
            packed.append(pltpu.roll(flank_s[side], (DIM - 32 * t) % DIM, 1) if t else flank_s[side])
    side_stat[...] = lax.dot_general(
        pick[...].astype(F32),
        jnp.concatenate(packed, axis=0),
        (((0,), (0,)), ((), ())),
        preferred_element_type=F32,
        precision=lax.Precision.HIGHEST,
    )
    spot = iota((TOKENS, DIM), 0) % PAD
    covered = (spot < RADIUS) | ((spot >= COLS - RADIUS) & (spot < COLS))
    wide_lane = iota((TOKENS, DIM), 1)

    def column(stat, where, index, fill):
        return jnp.max(jnp.where(where == index, stat, fill), axis=1, keepdims=True)

    def merge_flank(head, carry):
        at = lanes(head)
        stat = side_stat[...]
        m1 = jnp.where(covered, column(stat, wide_lane, head, LOW), LOW)
        l1 = jnp.where(covered, jnp.maximum(column(stat, wide_lane, head + HEADS, LOW), 0.0), 0.0)
        o1 = lax.dot_general(
            pick[...], flank_o[:, at], (((0,), (0,)), ((), ())), preferred_element_type=F32
        )
        m0 = own_m[head]
        top = jnp.maximum(m0, m1)
        a0, a1 = jnp.exp2(m0 - top), jnp.exp2(m1 - top)
        total = a0 * own_l[head] + a1 * l1
        mixed = a0 * own_o[head] + a1 * o1
        own_m[head] = top
        own_l[head] = total
        own_o[head] = mixed
        done = (mixed / total).astype(BF16)
        for r in range(RADIUS, ROWS - RADIUS):
            out_v[r, :, at] = done[r * PAD : r * PAD + COLS]
        return carry

    lax.fori_loop(0, HEADS, merge_flank, 0)
    middle = pl.ds(RADIUS, ROWS - 2 * RADIUS)
    store_middle = pltpu.make_async_copy(out_v.at[middle], out_hbm.at[middle], store_sem.at[0])
    store_middle.start()

    stores = []
    for turn in range(2):
        side = (turn + flip) % 2
        there = jnp.where(side == 0, has_up.astype(jnp.int32), has_down.astype(jnp.int32)) > 0
        device = (h - 1 + 2 * side, w)

        @pl.when(there)
        def _():
            for c in range(CHUNKS):
                copy_edge_o(1 - side, c, device).wait_recv()
            copy_edge_s(1 - side, device).wait_recv()

        part = pl.ds(pl.multiple_of(side * (TOKENS - EDGE), EDGE), EDGE)
        first = side * (ROWS - RADIUS)

        def merge_edge(head, carry):
            at = lanes(head)
            stat = edge_s[side]
            m1 = jnp.concatenate([column(stat, lane, 32 * t + head, LOW) for t in range(RADIUS)], axis=0)
            l1 = jnp.concatenate(
                [column(stat, lane, 32 * t + HEADS + head, LOW) for t in range(RADIUS)], axis=0
            )
            l1 = jnp.maximum(l1, 0.0)
            m0 = own_m[head, part]
            top = jnp.maximum(m0, m1)
            a0, a1 = jnp.exp2(m0 - top), jnp.exp2(m1 - top)
            total = a0 * own_l[head, part] + a1 * l1
            mixed = a0 * own_o[head, part] + a1 * edge_o[side, :, at].astype(F32)
            done = (mixed / total).astype(BF16)
            for t in range(RADIUS):
                out_v[first + t, :, at] = done[t * PAD : t * PAD + COLS]
            return carry

        lax.fori_loop(0, HEADS, merge_edge, 0)
        rows = pl.ds(first, RADIUS)
        store = pltpu.make_async_copy(out_v.at[rows], out_hbm.at[rows], store_sem.at[1 + turn])
        store.start()
        stores.append(store)

    for c in range(CHUNKS):
        @pl.when(has_down)
        def _():
            copy_q_edge(0, c, down).wait_send()
            copy_edge_o(1, c, down).wait_send()

        @pl.when(has_up)
        def _():
            copy_q_edge(1, c, up).wait_send()
            copy_edge_o(0, c, up).wait_send()

    @pl.when(has_down)
    def _():
        copy_edge_s(1, down).wait_send()

    @pl.when(has_up)
    def _():
        copy_edge_s(0, up).wait_send()

    for side, there, device in ((0, has_right, right), (1, has_left, left)):
        @pl.when(there)
        def _():
            copy_q_flank(side, device).wait_send()
            for s in range(2):
                copy_ext(side, s, device).wait_send()
            copy_flank_o(1 - side, device).wait_send()
            copy_flank_s(1 - side, device).wait_send()

    store_middle.wait()
    for store in stores:
        store.wait()


def on_device(nh, nw, queries, kv_new, kv_past):
    wide = HEADS * DIM
    span = EDGE + 2 * CORNER
    any_space = pl.BlockSpec(memory_space=pl.ANY)
    dma = pltpu.SemaphoreType.DMA
    return pl.pallas_call(
        functools.partial(kernel, nh, nw),
        out_shape=jax.ShapeDtypeStruct((ROWS, COLS, wide), BF16),
        in_specs=[any_space] * 3,
        out_specs=any_space,
        scratch_shapes=[
            pltpu.VMEM((ROWS, COLS, wide), BF16),
            pltpu.VMEM((2 * FRAMES, ROWS, COLS, wide), BF16),
            pltpu.VMEM((ROWS, COLS, wide), BF16),
            pltpu.VMEM((TOKENS, wide), BF16),
            pltpu.VMEM((2 * FRAMES, TOKENS, wide), BF16),
            pltpu.VMEM((2 * SIDE, wide), BF16),
            pltpu.VMEM((2 * FRAMES, 2 * SIDE, wide), BF16),
            pltpu.VMEM((2, EDGE, wide), BF16),
            pltpu.VMEM((2, SIDE, wide), BF16),
            pltpu.VMEM((2, 2 * FRAMES, 2 * CORNER, wide), BF16),
            pltpu.VMEM((HEADS, TOKENS, DIM), F32),
            pltpu.VMEM((HEADS, TOKENS, DIM), F32),
            pltpu.VMEM((HEADS, TOKENS, DIM), F32),
            pltpu.VMEM((4, SIDE, wide), BF16),
            pltpu.VMEM((4, PAD, DIM), F32),
            pltpu.VMEM((2, EDGE, wide), BF16),
            pltpu.VMEM((2, PAD, DIM), F32),
            pltpu.VMEM((2 * SIDE, wide), BF16),
            pltpu.VMEM((2, PAD, DIM), F32),
            pltpu.VMEM((TOKENS, TOKENS), F32),
            pltpu.VMEM((2, SIDE, FRAMES * SIDE), F32),
            pltpu.VMEM((2, EDGE, FRAMES * span), F32),
            pltpu.VMEM((2 * SIDE, TOKENS), BF16),
            pltpu.VMEM((TOKENS, DIM), F32),
            dma((1 + 2 * FRAMES,)),
            dma((3,)),
            dma((2, 2, CHUNKS)),
            dma((2, 2)),
            dma((2, 2, 2)),
            dma((2, 2, CHUNKS)),
            dma((2, 2)),
            dma((2, 4)),
        ],
        compiler_params=pltpu.CompilerParams(
            collective_id=0, has_side_effects=True, vmem_limit_bytes=48 * 1024 * 1024
        ),
    )(queries, kv_new, kv_past)


def solution(mesh):
    return jax.shard_map(
        functools.partial(on_device, mesh.shape["ha"], mesh.shape["wa"]),
        mesh=mesh,
        in_specs=(P("ha", "wa", None), P(None, "ha", "wa", None), P(None, None, "ha", "wa", None)),
        out_specs=P("ha", "wa", None),
        check_vma=False,
    )
```

time: 148 us -> 51.2 us (0.35)
  the two profiles are of different devices: /device:TPU:480 before, /device:TPU:31 now
where the time goes in v1:
time: 51.2 us; the launch traced here: 51 us
  Pallas kernels  45.8 us (89%)
  local copies, waits for them, and re-layouts  5.17 us (10%)
    pallas_call x1, Pallas kernels, on_device(): pl.pallas_call(functools.partial(kernel, nh, nw), out_shape=jax.ShapeDtyp...  45.8 us
    unnamed x5, local copies, waits for them, and re-layouts  4.15 us
    pallas_call x1, local copies, waits for them, and re-layouts, on_device(): pl.pallas_call(functools.partial(kernel, nh, nw), out_shape=jax.ShapeDtyp...  1.02 us

profile of v1, /device:TPU:31, one launch (start us, length us, event | category | flops | bytes accessed | tf_op | source)
XLA Modules:
  0.0 51.0 jit_solution(17288284225298276664)
XLA Ops:
  0.0 0.0 copy-start
  0.0 1.4 %copy.4.q_hbm = bf16[16,14,1024]{2,1,0:T(8,128)(2,1)S(1)} copy(bf16[16,14,1024]{2,0,1:T(8,128)(2,1)} %param.3) | data formatting | bytes 917504 | tf_op args[0]
  1.4 1.7 %copy.5.new_hbm = bf16[2,16,14,1024]{3,2,1,0:T(8,128)(2,1)S(1)} copy(bf16[2,16,14,1024]{3,1,2,0:T(8,128)(2,1)} %param.4) | data formatting | bytes 1835008 | tf_op args[1]
  3.1 0.0 copy-done
  3.1 1.0 %copy.6.past_hbm = bf16[2,2,16,14,1024]{4,3,2,1,0:T(8,128)(2,1)S(1)} copy(bf16[2,2,16,14,1024]{4,2,3,1,0:T(8,128)(2,1)S(1)} %copy-done) | data formatting | bytes 3670016 | tf_op args[2]
  4.2 45.8 %shard_map.37 = bf16[16,14,1024]{2,1,0:T(8,128)(2,1)S(1)} custom-call(bf16[16,14,1024]{2,1,0:T(8,128)(2,1)S(1)} %copy.4.q_hbm, bf16[2,16,14,1024]{3,2,1,0:T(8,128)(2,1)S(1)} %copy.5.new_hbm, bf16[2,2,16,14,1024]{4,3,2,1,0:T(8,128)(2,1)S(1)} %copy.6.past_hbm), custom_call_target="tpu_custom_call" | custom-call | tf_op jit(solution)/shard_map/pallas_call | solution.py:494
  50.0 1.0 %copy.7 = bf16[16,14,1024]{2,0,1:T(8,128)(2,1)} copy(bf16[16,14,1024]{2,1,0:T(8,128)(2,1)S(1)} %shard_map.37) | data formatting | bytes 917504 | tf_op jit(solution)/shard_map/pallas_call | solution.py:494
Async XLA Ops:
  0.0 3.1 %copy-start = (bf16[2,2,16,14,1024]{4,2,3,1,0:T(8,128)(2,1)S(1)}, bf16[2,2,16,14,1024]{4,2,3,1,0:T(8,128)(2,1)}, u32[]{:S(2)}) copy-start(bf16[2,2,16,14,1024]{4,2,3,1,0:T(8,128)(2,1)} %param.5) | copy-start | bytes 5505028

commit v2 on v1

v2 whole, which is shorter than its diff:
```python
import functools
import math

import jax
import jax.numpy as jnp
from jax import lax
from jax.experimental import pallas as pl
from jax.experimental.pallas import tpu as pltpu
from jax.sharding import PartitionSpec as P

MESH = pl.DeviceIdType.MESH
HEADS = 8
DIM = 128
RADIUS = 4
FRAMES = 3
ROWS = 16
COLS = 14
TOKENS = ROWS * COLS
FLANK = RADIUS * ROWS
SLOTS = 16
EDGE = SLOTS * RADIUS
CORNER = RADIUS * RADIUS
SPAN = EDGE + 2 * CORNER
GROUP = 16
CHUNKS = 4
LOW = -1e30
FOLD = math.log2(math.e) / math.sqrt(DIM)
F32 = jnp.float32
BF16 = jnp.bfloat16
CUT = 8 * ROWS
BLOCK1 = TOKENS - CUT
REACH0 = 12 * ROWS
REACH1 = 4 * ROWS
OWN_UNROLL = 8


def dot_nt(a, b):
    return lax.dot_general(a, b, (((1,), (1,)), ((), ())), preferred_element_type=F32)


def dot_nn(a, b):
    return lax.dot_general(a, b, (((1,), (0,)), ((), ())), preferred_element_type=F32)


def iota(shape, dim):
    return lax.broadcasted_iota(jnp.int32, shape, dim)


def lanes(head):
    if isinstance(head, int):
        return pl.ds(head * DIM, DIM)
    return pl.ds(pl.multiple_of(head * DIM, DIM), DIM)


def mask(allowed):
    return jnp.where(allowed, 0.0, LOW)


def edge_col(slot):
    return jnp.where(slot < COLS - RADIUS, slot, slot - (SLOTS - COLS))


def soft(scores, top):
    return jnp.exp2(scores * FOLD - top).astype(BF16)


def with_ones(values):
    return jnp.concatenate([values, jnp.ones_like(values)], axis=1)


def offset(scores):
    top = FOLD * jnp.max(scores, axis=1, keepdims=True)
    return top.astype(BF16).astype(F32)


def kernel(
    nh, nw,
    q_hbm, new_hbm, past_hbm, out,
    q_all, kv_all, q_pack, kv_pack,
    q_edge, q_flank, ext, own_o, own_m, own_l, edge_own_o, edge_own_m, edge_own_l,
    send_o, send_s, edge_o, edge_s, flank_o, flank_s,
    bias0, bias1, bias_flank, bias_edge, pick, spread,
    load_sem, q_edge_sem, q_flank_sem, ext_sem, edge_sem, flank_sem, stat_sem,
):
    h = lax.axis_index("ha")
    w = lax.axis_index("wa")
    has_up, has_down = h > 0, h < nh - 1
    has_left, has_right = w > 0, w < nw - 1
    up, down = (h - 1, w), (h + 1, w)
    left, right = (h, w - 1), (h, w + 1)
    flip = (h == nh // 2).astype(jnp.int32)

    barrier = pltpu.get_barrier_semaphore()
    for there, device in ((has_up, up), (has_down, down), (has_left, left), (has_right, right)):
        @pl.when(there)
        def _():
            pl.semaphore_signal(barrier, inc=1, device_id=device, device_id_type=MESH)

    loads = [pltpu.make_async_copy(q_hbm, q_all, load_sem.at[0])]
    for kv in range(2):
        for f in range(FRAMES):
            source = new_hbm.at[kv] if f == FRAMES - 1 else past_hbm.at[f, kv]
            slot = kv * FRAMES + f
            loads.append(pltpu.make_async_copy(source, kv_all.at[slot], load_sem.at[1 + slot]))
    for load in loads:
        load.start()

    def picked(shape, dim):
        i, t = iota(shape, dim), iota(shape, 1 - dim)
        slot = i % EDGE // RADIUS
        real = (slot < COLS - RADIUS) | (slot >= SLOTS - RADIUS)
        token = edge_col(slot) * ROWS + i % RADIUS + i // EDGE * (ROWS - RADIUS)
        return jnp.where(real & (t == token), 1.0, 0.0).astype(BF16)

    pick[...] = picked((2 * EDGE, TOKENS), 0)
    spread[...] = picked((TOKENS, 2 * EDGE), 1)

    for there, side in ((has_up, 0), (has_down, 1)):
        @pl.when(jnp.logical_not(there))
        def _():
            q_edge[side] = jnp.zeros(q_edge.shape[1:], BF16)
            edge_o[side] = jnp.zeros(edge_o.shape[1:], BF16)
            edge_s[side] = jnp.full(edge_s.shape[1:], LOW, F32)
    for there, side in ((has_left, 0), (has_right, 1)):
        @pl.when(jnp.logical_not(there))
        def _():
            q_flank[side] = jnp.zeros(q_flank.shape[1:], BF16)
            flank_o[side] = jnp.zeros(flank_o.shape[1:], BF16)
            flank_s[side] = jnp.full(flank_s.shape[1:], LOW, F32)
            for s in range(2):
                ext[s, :, side * CORNER : (side + 1) * CORNER, :] = jnp.zeros(
                    (2 * FRAMES, CORNER, HEADS * DIM), BF16
                )

    loads[0].wait()
    q_pack[...] = dot_nn(pick[...], q_all[...]).astype(BF16)

    def remote(src, dst, sems, index, device):
        return pltpu.make_async_remote_copy(
            src_ref=src,
            dst_ref=dst,
            send_sem=sems.at[(0, *index)],
            recv_sem=sems.at[(1, *index)],
            device_id=device,
            device_id_type=MESH,
        )

    width = HEADS * DIM // CHUNKS

    def copy_q_edge(side, c, device):
        part = pl.ds(c * width, width)
        return remote(
            q_pack.at[pl.ds((1 - side) * EDGE, EDGE), part],
            q_edge.at[side, :, part],
            q_edge_sem,
            (side, c),
            device,
        )

    def copy_q_flank(side, device):
        return remote(
            q_all.at[pl.ds((1 - side) * (TOKENS - FLANK), FLANK)],
            q_flank.at[side],
            q_flank_sem,
            (side,),
            device,
        )

    def copy_ext(side, s, device):
        return remote(
            kv_pack.at[:, pl.ds((1 - side) * (EDGE - CORNER) + s * EDGE, CORNER)],
            ext.at[s, :, pl.ds(side * CORNER, CORNER)],
            ext_sem,
            (side, s),
            device,
        )

    def copy_edge_o(side, c, device):
        part = pl.ds(c * width, width)
        return remote(
            send_o.at[side, :, part],
            edge_o.at[1 - side, :, part],
            edge_sem,
            (1 - side, c),
            device,
        )

    def copy_edge_s(side, device):
        return remote(send_s.at[side], edge_s.at[1 - side], stat_sem, (1 - side,), device)

    def copy_flank_o(side, device):
        return remote(send_o.at[2 + side], flank_o.at[1 - side], flank_sem, (1 - side,), device)

    def copy_flank_s(side, device):
        return remote(send_s.at[2 + side], flank_s.at[1 - side], stat_sem, (3 - side,), device)

    n_near = (
        has_up.astype(jnp.int32)
        + has_down.astype(jnp.int32)
        + has_left.astype(jnp.int32)
        + has_right.astype(jnp.int32)
    )
    pl.semaphore_wait(barrier, n_near)

    for c in range(CHUNKS):
        @pl.when(has_down)
        def _():
            copy_q_edge(0, c, down).start()

        @pl.when(has_up)
        def _():
            copy_q_edge(1, c, up).start()

    @pl.when(has_right)
    def _():
        copy_q_flank(0, right).start()

    @pl.when(has_left)
    def _():
        copy_q_flank(1, left).start()

    for slot in range(2 * FRAMES):
        loads[1 + slot].wait()
        kv_pack[slot] = dot_nn(pick[...], kv_all[slot]).astype(BF16)

    for s in range(2):
        @pl.when(has_right)
        def _():
            copy_ext(0, s, right).start()

        @pl.when(has_left)
        def _():
            copy_ext(1, s, left).start()

    q, k = iota(bias0.shape, 0), iota(bias0.shape, 1)
    bias0[...] = mask((abs(q // ROWS - k // ROWS) <= RADIUS) & (abs(q % ROWS - k % ROWS) <= RADIUS))
    q, k = iota(bias1.shape, 0) + REACH1, iota(bias1.shape, 1) + BLOCK1
    bias1[...] = mask(
        (abs(q // ROWS - k // ROWS) <= RADIUS) & (abs(q % ROWS - k % ROWS) <= RADIUS) & (k >= CUT)
    )

    q, k = iota(bias_flank.shape[1:], 0), iota(bias_flank.shape[1:], 1)
    rows_near = (abs(q % ROWS - k % ROWS) <= RADIUS) & (k < FRAMES * FLANK)
    k = k % FLANK
    bias_flank[0] = mask(rows_near & (k // ROWS <= q // ROWS))
    bias_flank[1] = mask(rows_near & (k // ROWS >= q // ROWS))

    q, k = iota((EDGE, FRAMES * SPAN), 0), iota((EDGE, FRAMES * SPAN), 1) % SPAN
    slot = k // RADIUS
    in_left = (k >= EDGE) & (k < EDGE + CORNER)
    in_right = k >= EDGE + CORNER
    key_col = jnp.where(
        in_left, slot - SLOTS - RADIUS, jnp.where(in_right, slot - SLOTS - RADIUS + COLS, edge_col(slot))
    )
    real = jnp.where(
        in_left,
        has_left.astype(jnp.int32),
        jnp.where(
            in_right,
            has_right.astype(jnp.int32),
            ((slot < COLS - RADIUS) | (slot >= SLOTS - RADIUS)).astype(jnp.int32),
        ),
    )
    cols_near = (abs(edge_col(q // RADIUS) - key_col) <= RADIUS) & (real > 0)
    bias_edge[0] = mask(cols_near & (k % RADIUS <= q % RADIUS))
    bias_edge[1] = mask(cols_near & (k % RADIUS >= q % RADIUS))

    def own_head(head):
        at = lanes(head)

        def block(kv, first, size):
            return jnp.concatenate(
                [kv_all[kv * FRAMES + f, pl.ds(first, size), at] for f in range(FRAMES)], axis=0
            )

        s0 = dot_nt(q_all[0:REACH0, at], block(0, 0, CUT)) + jnp.concatenate(
            [bias0[...]] * FRAMES, axis=1
        )
        s1 = dot_nt(q_all[REACH1:TOKENS, at], block(0, BLOCK1, CUT)) + jnp.concatenate(
            [bias1[...]] * FRAMES, axis=1
        )
        t0 = jnp.max(s0, axis=1, keepdims=True)
        t1 = jnp.max(s1, axis=1, keepdims=True)
        both = REACH0 - REACH1
        top = FOLD * jnp.concatenate(
            [t0[0:REACH1], jnp.maximum(t0[REACH1:], t1[0:both]), t1[both:]], axis=0
        )
        top = top.astype(BF16).astype(F32)
        o0 = dot_nn(soft(s0, top[0:REACH0]), with_ones(block(1, 0, CUT)))
        o1 = dot_nn(soft(s1, top[REACH1:TOKENS]), with_ones(block(1, BLOCK1, CUT)))
        o = jnp.concatenate([o0[0:REACH1], o0[REACH1:] + o1[0:both], o1[both:]], axis=0)
        own_o[head] = o[:, :DIM]
        own_l[head] = o[:, DIM:]
        own_m[head] = jnp.broadcast_to(top, (TOKENS, DIM))

    def own_heads(i, carry):
        for j in range(OWN_UNROLL):
            own_head(i * OWN_UNROLL + j)
        return carry

    lax.fori_loop(0, HEADS // OWN_UNROLL, own_heads, 0)

    lane = iota((GROUP, DIM), 1)

    def guest(head, stat, q, k, v, bias):
        s = dot_nt(q, k) + bias
        top = offset(s)
        o = dot_nn(soft(s, top), with_ones(v))
        for t in range(4):
            rows = slice(t * GROUP, (t + 1) * GROUP)
            stat = jnp.where(lane == 32 * t + head, top[rows], stat)
            stat = jnp.where(lane == 32 * t + HEADS + head, o[rows, DIM:], stat)
        return o[:, :DIM].astype(BF16), stat

    sides = ((0, has_left, left), (1, has_right, right))
    for side, there, device in sides:
        @pl.when(there)
        def _():
            copy_q_flank(side, device).wait_recv()

    stats = [jnp.zeros((GROUP, DIM), F32)] * 2
    for head in range(HEADS):
        at = lanes(head)
        for side in range(2):
            part = pl.ds(side * (TOKENS - FLANK), FLANK)
            k = jnp.concatenate([kv_all[f, part, at] for f in (0, 1, 2, 0)], axis=0)
            v = jnp.concatenate([kv_all[FRAMES + f, part, at] for f in (0, 1, 2, 0)], axis=0)
            o, stats[side] = guest(head, stats[side], q_flank[side, :, at], k, v, bias_flank[side])
            send_o[2 + side, :, at] = o
    for side, there, device in sides:
        send_s[2 + side] = stats[side]

        @pl.when(there)
        def _():
            copy_flank_o(side, device).start()
            copy_flank_s(side, device).start()

    for side, there, device in sides:
        @pl.when(there)
        def _():
            for s in range(2):
                copy_ext(side, s, device).wait_recv()

    def edge_head(side, head, stat):
        at = lanes(head)
        part = pl.ds(pl.multiple_of(side * EDGE, EDGE), EDGE)

        def keys(kv):
            pieces = []
            for f in range(FRAMES):
                pieces.append(kv_pack[kv * FRAMES + f, part, at])
                pieces.append(ext[side, kv * FRAMES + f, :, at])
            return jnp.concatenate(pieces, axis=0)

        o, stat = guest(head, stat, q_edge[side, :, at], keys(0), keys(1), bias_edge[side])
        send_o[side, :, at] = o
        return stat

    def edge_of(turn):
        side = (turn + flip) % 2
        there = jnp.where(side == 0, has_up.astype(jnp.int32), has_down.astype(jnp.int32)) > 0
        return side, there, (h - 1 + 2 * side, w)

    per = HEADS // CHUNKS
    side, there, device = edge_of(0)

    @pl.when(there)
    def _():
        for c in range(CHUNKS):
            copy_q_edge(side, c, device).wait_recv()
        stat = jnp.zeros((GROUP, DIM), F32)
        for head in range(HEADS):
            stat = edge_head(side, head, stat)
        send_s[side] = stat
        for c in range(CHUNKS):
            copy_edge_o(side, c, device).start()
        copy_edge_s(side, device).start()

    side1, there1, device1 = edge_of(1)

    @pl.when(there1)
    def _():
        stat = jnp.zeros((GROUP, DIM), F32)
        for c in range(CHUNKS):
            copy_q_edge(side1, c, device1).wait_recv()
            for i in range(per):
                stat = edge_head(side1, c * per + i, stat)
            copy_edge_o(side1, c, device1).start()
        send_s[side1] = stat
        copy_edge_s(side1, device1).start()

    for side, there, device in sides:
        @pl.when(there)
        def _():
            copy_flank_o(1 - side, device).wait_recv()
            copy_flank_s(1 - side, device).wait_recv()

    def column(stat, index):
        return jnp.concatenate(
            [stat[:, 32 * t + index : 32 * t + index + 1] for t in range(4)], axis=0
        )

    def merge(own, other):
        (m0, l0, o0), (m1, l1, o1) = own, other
        top = jnp.maximum(m0, m1)
        a0, a1 = jnp.exp2(m0 - top), jnp.exp2(m1 - top)
        return top, a0 * l0 + a1 * jnp.maximum(l1, 0.0), a0 * o0 + a1 * o1.astype(F32)

    wide_lane = iota((TOKENS, DIM), 1)
    own_stat = jnp.zeros((TOKENS, DIM), F32)
    for head in range(HEADS):
        at = lanes(head)
        for side in range(2):
            part = pl.ds(side * (TOKENS - FLANK), FLANK)
            stat = flank_s[side]
            top, total, mixed = merge(
                (own_m[head, part], own_l[head, part], own_o[head, part]),
                (column(stat, head), column(stat, HEADS + head), flank_o[side, :, at]),
            )
            own_m[head, part] = top
            own_l[head, part] = total
            own_o[head, part] = mixed
        total = own_l[head]
        high = total.astype(BF16).astype(F32)
        own_stat = jnp.where(wide_lane == head, own_m[head], own_stat)
        own_stat = jnp.where(wide_lane == HEADS + head, high, own_stat)
        own_stat = jnp.where(wide_lane == 2 * HEADS + head, total - high, own_stat)
    packed_stat = dot_nn(pick[...], own_stat.astype(BF16))
    inner = iota((TOKENS, DIM), 0) % ROWS
    inner = (inner >= RADIUS) & (inner < ROWS - RADIUS)
    for head in range(HEADS):
        at = lanes(head)
        o = own_o[head]
        high = o.astype(BF16)
        rest = (o - high.astype(F32)).astype(BF16)
        edge_own_o[head] = dot_nn(pick[...], high) + dot_nn(pick[...], rest)
        edge_own_m[head] = jnp.broadcast_to(packed_stat[:, head : head + 1], (2 * EDGE, DIM))
        edge_own_l[head] = jnp.broadcast_to(
            packed_stat[:, HEADS + head : HEADS + head + 1]
            + packed_stat[:, 2 * HEADS + head : 2 * HEADS + head + 1],
            (2 * EDGE, DIM),
        )
        out[:, at] = jnp.where(inner, o / own_l[head], 0.0).astype(BF16)

    for turn in range(2):
        side, there, device = edge_of(turn)

        @pl.when(there)
        def _():
            for c in range(CHUNKS):
                copy_edge_o(1 - side, c, device).wait_recv()
            copy_edge_s(1 - side, device).wait_recv()

        part = pl.ds(pl.multiple_of(side * EDGE, EDGE), EDGE)
        stat = edge_s[side]
        slot = iota((EDGE, DIM), 0) // RADIUS
        real = (slot < COLS - RADIUS) | (slot >= SLOTS - RADIUS)
        place = jnp.where(side == 0, spread[:, 0:EDGE], spread[:, EDGE : 2 * EDGE])
        for head in range(HEADS):
            at = lanes(head)
            top, total, mixed = merge(
                (edge_own_m[head, part], edge_own_l[head, part], edge_own_o[head, part]),
                (column(stat, head), column(stat, HEADS + head), edge_o[side, :, at]),
            )
            done = jnp.where(real, mixed / total, 0.0).astype(BF16)
            out[:, at] = (out[:, at].astype(F32) + dot_nn(place, done)).astype(BF16)

    for c in range(CHUNKS):
        @pl.when(has_down)
        def _():
            copy_q_edge(0, c, down).wait_send()
            copy_edge_o(1, c, down).wait_send()

        @pl.when(has_up)
        def _():
            copy_q_edge(1, c, up).wait_send()
            copy_edge_o(0, c, up).wait_send()

    @pl.when(has_down)
    def _():
        copy_edge_s(1, down).wait_send()

    @pl.when(has_up)
    def _():
        copy_edge_s(0, up).wait_send()

    for side, there, device in ((0, has_right, right), (1, has_left, left)):
        @pl.when(there)
        def _():
            copy_q_flank(side, device).wait_send()
            for s in range(2):
                copy_ext(side, s, device).wait_send()
            copy_flank_o(1 - side, device).wait_send()
            copy_flank_s(1 - side, device).wait_send()


def on_device(nh, nw, queries, kv_new, kv_past):
    wide = HEADS * DIM
    hbm = pl.BlockSpec(memory_space=pltpu.HBM)
    dma = pltpu.SemaphoreType.DMA
    queries = queries.transpose(1, 0, 2).reshape(TOKENS, wide)
    kv_new = kv_new.transpose(0, 2, 1, 3).reshape(2, TOKENS, wide)
    kv_past = kv_past.transpose(0, 1, 3, 2, 4).reshape(FRAMES - 1, 2, TOKENS, wide)
    out = pl.pallas_call(
        functools.partial(kernel, nh, nw),
        out_shape=jax.ShapeDtypeStruct((TOKENS, wide), BF16),
        in_specs=[hbm] * 3,
        out_specs=pl.BlockSpec(memory_space=pltpu.VMEM),
        scratch_shapes=[
            pltpu.VMEM((TOKENS, wide), BF16),
            pltpu.VMEM((2 * FRAMES, TOKENS, wide), BF16),
            pltpu.VMEM((2 * EDGE, wide), BF16),
            pltpu.VMEM((2 * FRAMES, 2 * EDGE, wide), BF16),
            pltpu.VMEM((2, EDGE, wide), BF16),
            pltpu.VMEM((2, FLANK, wide), BF16),
            pltpu.VMEM((2, 2 * FRAMES, 2 * CORNER, wide), BF16),
            pltpu.VMEM((HEADS, TOKENS, DIM), F32),
            pltpu.VMEM((HEADS, TOKENS, DIM), F32),
            pltpu.VMEM((HEADS, TOKENS, DIM), F32),
            pltpu.VMEM((HEADS, 2 * EDGE, DIM), F32),
            pltpu.VMEM((HEADS, 2 * EDGE, DIM), F32),
            pltpu.VMEM((HEADS, 2 * EDGE, DIM), F32),
            pltpu.VMEM((4, EDGE, wide), BF16),
            pltpu.VMEM((4, GROUP, DIM), F32),
            pltpu.VMEM((2, EDGE, wide), BF16),
            pltpu.VMEM((2, GROUP, DIM), F32),
            pltpu.VMEM((2, FLANK, wide), BF16),
            pltpu.VMEM((2, GROUP, DIM), F32),
            pltpu.VMEM((REACH0, CUT), F32),
            pltpu.VMEM((TOKENS - REACH1, CUT), F32),
            pltpu.VMEM((2, FLANK, (FRAMES + 1) * FLANK), F32),
            pltpu.VMEM((2, EDGE, FRAMES * SPAN), F32),
            pltpu.VMEM((2 * EDGE, TOKENS), BF16),
            pltpu.VMEM((TOKENS, 2 * EDGE), BF16),
            dma((1 + 2 * FRAMES,)),
            dma((2, 2, CHUNKS)),
            dma((2, 2)),
            dma((2, 2, 2)),
            dma((2, 2, CHUNKS)),
            dma((2, 2)),
            dma((2, 4)),
        ],
        compiler_params=pltpu.CompilerParams(
            collective_id=0, has_side_effects=True, vmem_limit_bytes=60 * 1024 * 1024
        ),
    )(queries, kv_new, kv_past)
    return out.reshape(COLS, ROWS, wide).transpose(1, 0, 2)


def solution(mesh):
    return jax.shard_map(
        functools.partial(on_device, mesh.shape["ha"], mesh.shape["wa"]),
        mesh=mesh,
        in_specs=(P("ha", "wa", None), P(None, "ha", "wa", None), P(None, None, "ha", "wa", None)),
        out_specs=P("ha", "wa", None),
        check_vma=False,
    )
```

time: 51.2 us -> 46.3 us (0.904)
  local copies, waits for them, and re-layouts: 5.17 us -> 1.82 us
  Pallas kernels: 45.8 us -> 44.3 us
    unnamed x5 -> x1, local copies, waits for them, and re-layouts: 4.15 us -> 1.82 us
    pallas_call x1, Pallas kernels: 45.8 us -> 44.3 us  [on_device(): pl.pallas_call(functools.partial(kernel, nh, nw), out_shape=jax.ShapeDtyp...]
    pallas_call x1 -> x0, local copies, waits for them, and re-layouts: 1.02 us -> none  [on_device(): pl.pallas_call(functools.partial(kernel, nh, nw), out_shape=jax.ShapeDtyp...]
where the time goes in v2:
time: 46.3 us; the launch traced here: 46.2 us
  Pallas kernels  44.3 us (96%)
  local copies, waits for them, and re-layouts  1.82 us (4%)
    pallas_call x1, Pallas kernels, on_device(): pl.pallas_call(functools.partial(kernel, nh, nw), out_shape=jax.ShapeDtyp...  44.3 us
    unnamed x1, local copies, waits for them, and re-layouts  1.82 us

profile of v2, /device:TPU:31, one launch (start us, length us, event | category | flops | bytes accessed | tf_op | source)
XLA Modules:
  0.0 46.2 jit_solution(15191187253407475957)
XLA Ops:
  0.0 44.3 %shard_map.37 = bf16[224,1024]{1,0:T(8,128)(2,1)} custom-call(bf16[224,1024]{1,0:T(8,128)(2,1)} %bitcast.15, bf16[2,224,1024]{2,1,0:T(8,128)(2,1)} %bitcast.14, bf16[2,2,224,1024]{3,2,1,0:T(8,128)(2,1)} %bitcast.13), custom_call_target="tpu_custom_call" | custom-call | tf_op jit(solution)/shard_map/pallas_call | solution.py:504
  44.3 1.8 %copy.5 = bf16[16,14,1024]{2,0,1:T(8,128)(2,1)} copy(bf16[16,14,1024]{2,0,1:T(8,128)(2,1)} %bitcast.12) | data formatting | bytes 917504

commit v3 on v2

--- a/solution.py
+++ b/solution.py
@@ -21,9 +21,11 @@
 EDGE = SLOTS * RADIUS
 CORNER = RADIUS * RADIUS
 SPAN = EDGE + 2 * CORNER
+CORNERS = 4
 GROUP = 16
-CHUNKS = 4
+CHUNKS = 2
 LOW = -1e30
+VMEM_BYTES = 54579 * 1024
 FOLD = math.log2(math.e) / math.sqrt(DIM)
 F32 = jnp.float32
 BF16 = jnp.bfloat16
@@ -77,10 +79,12 @@
     nh, nw,
     q_hbm, new_hbm, past_hbm, out,
     q_all, kv_all, q_pack, kv_pack,
-    q_edge, q_flank, ext, own_o, own_m, own_l, edge_own_o, edge_own_m, edge_own_l,
-    send_o, send_s, edge_o, edge_s, flank_o, flank_s,
-    bias0, bias1, bias_flank, bias_edge, pick, spread,
-    load_sem, q_edge_sem, q_flank_sem, ext_sem, edge_sem, flank_sem, stat_sem,
+    q_edge, q_flank, q_corner, ext, own_o, own_m, own_l, edge_own_o, edge_own_m, edge_own_l,
+    send_o, send_s, edge_o, edge_s, flank_o, flank_s, corner_o, corner_s,
+    via_q, via_o, via_s,
+    bias0, bias1, bias_flank, bias_near, bias_far, bias_corner, pick, spread,
+    load_sem, q_edge_sem, q_flank_sem, q_corner_sem, ext_sem,
+    edge_sem, flank_sem, corner_sem, stat_sem, via_sem, onward_sem,
 ):
     h = lax.axis_index("ha")
     w = lax.axis_index("wa")
@@ -89,9 +93,32 @@
     up, down = (h - 1, w), (h + 1, w)
     left, right = (h, w - 1), (h, w + 1)
     flip = (h == nh // 2).astype(jnp.int32)
+    far_up, far_down = h == nh // 2, h == nh // 2 - 1
+    far = far_up | far_down
+    near_up, near_down = has_up & (h != nh // 2), has_down & (h != nh // 2 - 1)
+    corners = (
+        (near_up & has_left, (h - 1, w - 1)),
+        (near_up & has_right, (h - 1, w + 1)),
+        (near_down & has_left, (h + 1, w - 1)),
+        (near_down & has_right, (h + 1, w + 1)),
+    )
+    near = ((near_up, up), (near_down, down), (has_left, left), (has_right, right)) + corners
+
+    relayed = (w >= nw // 2) & ((w // 4 - nw // 8) % 2 == 1)
+    via_down, via_up = nh // 2 + 2, nh // 2 - 3
+    serves_down, serves_up = relayed & (h == via_down), relayed & (h == via_up)
+    serves = serves_down | serves_up
+    far_side = serves_up.astype(jnp.int32)
+    served, target = (nh // 2 - 1 + far_side, w), (nh // 2 - far_side, w)
+    my_via = (jnp.where(far_down, via_down, via_up), w)
+    other_via = (jnp.where(far_down, via_up, via_down), w)
+    far_via, far_direct = far & relayed, far & jnp.logical_not(relayed)
+    across = (nh // 2 - flip, w)
+    greet = near + ((far_via, other_via), (far_direct, across), (serves, served))
+    awaited = [there for there, _ in near] + [far, serves]
 
     barrier = pltpu.get_barrier_semaphore()
-    for there, device in ((has_up, up), (has_down, down), (has_left, left), (has_right, right)):
+    for there, device in greet:
         @pl.when(there)
         def _():
             pl.semaphore_signal(barrier, inc=1, device_id=device, device_id_type=MESH)
@@ -127,10 +154,19 @@
             q_flank[side] = jnp.zeros(q_flank.shape[1:], BF16)
             flank_o[side] = jnp.zeros(flank_o.shape[1:], BF16)
             flank_s[side] = jnp.full(flank_s.shape[1:], LOW, F32)
-            for s in range(2):
-                ext[s, :, side * CORNER : (side + 1) * CORNER, :] = jnp.zeros(
-                    (2 * FRAMES, CORNER, HEADS * DIM), BF16
-                )
+
+        @pl.when(jnp.logical_not(there & far))
+        def _():
+            ext[:, side * CORNER : (side + 1) * CORNER, :] = jnp.zeros(
+                (2 * FRAMES, CORNER, HEADS * DIM), BF16
+            )
+    for t, (there, _) in enumerate(corners):
+        @pl.when(jnp.logical_not(there))
+        def _():
+            rows = slice(t * CORNER, (t + 1) * CORNER)
+            q_corner[rows, :] = jnp.zeros((CORNER, HEADS * DIM), BF16)
+            corner_o[rows, :] = jnp.zeros((CORNER, HEADS * DIM), BF16)
+            corner_s[t] = jnp.full(corner_s.shape[1:], LOW, F32)
 
     loads[0].wait()
     q_pack[...] = dot_nn(pick[...], q_all[...]).astype(BF16)
@@ -166,12 +202,25 @@
             device,
         )
 
-    def copy_ext(side, s, device):
+    def corner_rows(t):
+        return pl.ds(t // 2 * EDGE + t % 2 * (EDGE - CORNER), CORNER)
+
+    def copy_q_corner(t, device):
         return remote(
-            kv_pack.at[:, pl.ds((1 - side) * (EDGE - CORNER) + s * EDGE, CORNER)],
-            ext.at[s, :, pl.ds(side * CORNER, CORNER)],
+            q_pack.at[corner_rows(t)],
+            q_corner.at[pl.ds((CORNERS - 1 - t) * CORNER, CORNER)],
+            q_corner_sem,
+            (CORNERS - 1 - t,),
+            device,
+        )
+
+    def copy_ext(side, device):
+        start = (1 - side) * (EDGE - CORNER) + (1 - flip) * EDGE
+        return remote(
+            kv_pack.at[:, pl.ds(pl.multiple_of(start, CORNER), CORNER)],
+            ext.at[:, pl.ds(side * CORNER, CORNER)],
             ext_sem,
-            (side, s),
+            (side,),
             device,
         )
 
@@ -194,20 +243,87 @@
     def copy_flank_s(side, device):
         return remote(send_s.at[2 + side], flank_s.at[1 - side], stat_sem, (3 - side,), device)
 
-    n_near = (
-        has_up.astype(jnp.int32)
-        + has_down.astype(jnp.int32)
-        + has_left.astype(jnp.int32)
-        + has_right.astype(jnp.int32)
-    )
-    pl.semaphore_wait(barrier, n_near)
+    def copy_corner_o(t, device):
+        return remote(
+            send_o.at[4, pl.ds(t * CORNER, CORNER)],
+            corner_o.at[pl.ds((CORNERS - 1 - t) * CORNER, CORNER)],
+            corner_sem,
+            (CORNERS - 1 - t,),
+            device,
+        )
+
+    def copy_corner_s(t, device):
+        return remote(
+            send_s.at[4], corner_s.at[CORNERS - 1 - t], stat_sem, (7 - t,), device
+        )
+
+    def to_via(src, dst, index):
+        return remote(src, dst, via_sem, (index,), my_via)
+
+    def onward(src, dst, index, there_sem):
+        return pltpu.make_async_remote_copy(
+            src_ref=src,
+            dst_ref=dst,
+            send_sem=onward_sem.at[index],
+            recv_sem=there_sem,
+            device_id=target,
+            device_id_type=MESH,
+        )
+
+    def to_via_q(c):
+        part = pl.ds(c * width, width)
+        start = pl.multiple_of((1 - flip) * EDGE, EDGE)
+        return to_via(q_pack.at[pl.ds(start, EDGE), part], via_q.at[:, part], c)
+
+    def far_q(c):
+        part = pl.ds(c * width, width)
+        start = pl.multiple_of((1 - flip) * EDGE, EDGE)
+        return remote(
+            q_pack.at[pl.ds(start, EDGE), part],
+            q_edge.at[flip, :, part],
+            q_edge_sem,
+            (flip, c),
+            across,
+        )
+
+    def to_via_o(c):
+        part = pl.ds(c * width, width)
+        return to_via(send_o.at[1 - flip, :, part], via_o.at[:, part], CHUNKS + c)
+
+    def to_via_s():
+        return to_via(send_s.at[1 - flip], via_s, 2 * CHUNKS)
+
+    def onward_q(c):
+        part = pl.ds(c * width, width)
+        return onward(
+            via_q.at[:, part], q_edge.at[far_side, :, part], c, q_edge_sem.at[1, far_side, c]
+        )
+
+    def onward_o(c):
+        part = pl.ds(c * width, width)
+        return onward(
+            via_o.at[:, part], edge_o.at[far_side, :, part], CHUNKS + c, edge_sem.at[1, far_side, c]
+        )
+
+    def onward_s():
+        return onward(via_s, edge_s.at[far_side], 2 * CHUNKS, stat_sem.at[1, far_side])
+
+    pl.semaphore_wait(barrier, sum(there.astype(jnp.int32) for there in awaited))
 
     for c in range(CHUNKS):
-        @pl.when(has_down)
+        @pl.when(far_via)
+        def _():
+            to_via_q(c).start()
+
+        @pl.when(far_direct)
+        def _():
+            far_q(c).start()
+
+        @pl.when(near_down)
         def _():
             copy_q_edge(0, c, down).start()
 
-        @pl.when(has_up)
+        @pl.when(near_up)
         def _():
             copy_q_edge(1, c, up).start()
 
@@ -218,19 +334,23 @@
     @pl.when(has_left)
     def _():
         copy_q_flank(1, left).start()
+
+    for t, (there, device) in enumerate(corners):
+        @pl.when(there)
+        def _():
+            copy_q_corner(t, device).start()
 
     for slot in range(2 * FRAMES):
         loads[1 + slot].wait()
         kv_pack[slot] = dot_nn(pick[...], kv_all[slot]).astype(BF16)
 
-    for s in range(2):
-        @pl.when(has_right)
-        def _():
-            copy_ext(0, s, right).start()
-
-        @pl.when(has_left)
-        def _():
-            copy_ext(1, s, left).start()
+    @pl.when(far & has_right)
+    def _():
+        copy_ext(0, right).start()
+
+    @pl.when(far & has_left)
+    def _():
+        copy_ext(1, left).start()
 
     q, k = iota(bias0.shape, 0), iota(bias0.shape, 1)
     bias0[...] = mask((abs(q // ROWS - k // ROWS) <= RADIUS) & (abs(q % ROWS - k % ROWS) <= RADIUS))
@@ -245,7 +365,17 @@
     bias_flank[0] = mask(rows_near & (k // ROWS <= q // ROWS))
     bias_flank[1] = mask(rows_near & (k // ROWS >= q // ROWS))
 
-    q, k = iota((EDGE, FRAMES * SPAN), 0), iota((EDGE, FRAMES * SPAN), 1) % SPAN
+    def real_slot(slot):
+        return (slot < COLS - RADIUS) | (slot >= SLOTS - RADIUS)
+
+    q, k = iota(bias_near.shape[1:], 0), iota(bias_near.shape[1:], 1)
+    slot = k % EDGE // RADIUS
+    cols_near = abs(edge_col(q // RADIUS) - edge_col(slot)) <= RADIUS
+    cols_near = cols_near & real_slot(slot) & (k < FRAMES * EDGE)
+    bias_near[0] = mask(cols_near & (k % RADIUS <= q % RADIUS))
+    bias_near[1] = mask(cols_near & (k % RADIUS >= q % RADIUS))
+
+    q, k = iota(bias_far.shape, 0), iota(bias_far.shape, 1) % SPAN
     slot = k // RADIUS
     in_left = (k >= EDGE) & (k < EDGE + CORNER)
     in_right = k >= EDGE + CORNER
@@ -254,16 +384,19 @@
     )
     real = jnp.where(
         in_left,
-        has_left.astype(jnp.int32),
-        jnp.where(
-            in_right,
-            has_right.astype(jnp.int32),
-            ((slot < COLS - RADIUS) | (slot >= SLOTS - RADIUS)).astype(jnp.int32),
-        ),
+        (far & has_left).astype(jnp.int32),
+        jnp.where(in_right, (far & has_right).astype(jnp.int32), real_slot(slot).astype(jnp.int32)),
     )
-    cols_near = (abs(edge_col(q // RADIUS) - key_col) <= RADIUS) & (real > 0)
-    bias_edge[0] = mask(cols_near & (k % RADIUS <= q % RADIUS))
-    bias_edge[1] = mask(cols_near & (k % RADIUS >= q % RADIUS))
+    sign = 2 * flip - 1
+    rows_near = (q % RADIUS - k % RADIUS) * sign >= 0
+    bias_far[...] = mask((abs(edge_col(q // RADIUS) - key_col) <= RADIUS) & (real > 0) & rows_near)
+
+    q, k = iota(bias_corner.shape, 0), iota(bias_corner.shape, 1)
+    same = (q // CORNER == k % EDGE // CORNER) & (k < FRAMES * EDGE)
+    down_sign, right_sign = 1 - q // CORNER // 2 * 2, 1 - q // CORNER % 2 * 2
+    rows_near = (q % RADIUS - k % RADIUS) * down_sign >= 0
+    cols_near = (q % CORNER // RADIUS - k % CORNER // RADIUS) * right_sign >= 0
+    bias_corner[...] = mask(same & rows_near & cols_near)
 
     def own_head(head):
         at = lanes(head)
@@ -335,13 +468,16 @@
             copy_flank_o(side, device).start()
             copy_flank_s(side, device).start()
 
-    for side, there, device in sides:
-        @pl.when(there)
-        def _():
-            for s in range(2):
-                copy_ext(side, s, device).wait_recv()
-
-    def edge_head(side, head, stat):
+    def near_head(side, head, stat):
+        at = lanes(head)
+        part = pl.ds(pl.multiple_of(side * EDGE, EDGE), EDGE)
+        k = jnp.concatenate([kv_pack[f, part, at] for f in (0, 1, 2, 0)], axis=0)
+        v = jnp.concatenate([kv_pack[FRAMES + f, part, at] for f in (0, 1, 2, 0)], axis=0)
+        o, stat = guest(head, stat, q_edge[side, :, at], k, v, bias_near[side])
+        send_o[side, :, at] = o
+        return stat
+
+    def far_head(side, head, stat):
         at = lanes(head)
         part = pl.ds(pl.multiple_of(side * EDGE, EDGE), EDGE)
 
@@ -349,10 +485,10 @@
             pieces = []
             for f in range(FRAMES):
                 pieces.append(kv_pack[kv * FRAMES + f, part, at])
-                pieces.append(ext[side, kv * FRAMES + f, :, at])
+                pieces.append(ext[kv * FRAMES + f, :, at])
             return jnp.concatenate(pieces, axis=0)
 
-        o, stat = guest(head, stat, q_edge[side, :, at], keys(0), keys(1), bias_edge[side])
+        o, stat = guest(head, stat, q_edge[side, :, at], keys(0), keys(1), bias_far[...])
         send_o[side, :, at] = o
         return stat
 
@@ -370,12 +506,44 @@
             copy_q_edge(side, c, device).wait_recv()
         stat = jnp.zeros((GROUP, DIM), F32)
         for head in range(HEADS):
-            stat = edge_head(side, head, stat)
+            stat = near_head(side, head, stat)
         send_s[side] = stat
         for c in range(CHUNKS):
             copy_edge_o(side, c, device).start()
         copy_edge_s(side, device).start()
 
+    for t, (there, device) in enumerate(corners):
+        @pl.when(there)
+        def _():
+            copy_q_corner(CORNERS - 1 - t, device).wait_recv()
+
+    stat = jnp.zeros((GROUP, DIM), F32)
+    for head in range(HEADS):
+        at = lanes(head)
+
+        def corner_keys(kv):
+            pieces = []
+            for f in (0, 1, 2, 0):
+                for t in range(CORNERS):
+                    pieces.append(kv_pack[kv * FRAMES + f, corner_rows(t), at])
+            return jnp.concatenate(pieces, axis=0)
+
+        o, stat = guest(
+            head, stat, q_corner[:, at], corner_keys(0), corner_keys(1), bias_corner[...]
+        )
+        send_o[4, :, at] = o
+    send_s[4] = stat
+    for t, (there, device) in enumerate(corners):
+        @pl.when(there)
+        def _():
+            copy_corner_o(t, device).start()
+            copy_corner_s(t, device).start()
+
+    for side, there, device in sides:
+        @pl.when(there & far)
+        def _():
+            copy_ext(side, device).wait_recv()
+
     side1, there1, device1 = edge_of(1)
 
     @pl.when(there1)
@@ -384,10 +552,31 @@
         for c in range(CHUNKS):
             copy_q_edge(side1, c, device1).wait_recv()
             for i in range(per):
-                stat = edge_head(side1, c * per + i, stat)
-            copy_edge_o(side1, c, device1).start()
+                stat = far_head(side1, c * per + i, stat)
+
+            @pl.when(far_via)
+            def _():
+                to_via_o(c).start()
+
+            @pl.when(jnp.logical_not(far_via))
+            def _():
+                copy_edge_o(side1, c, device1).start()
+
         send_s[side1] = stat
-        copy_edge_s(side1, device1).start()
+
+        @pl.when(far_via)
+        def _():
+            to_via_s().start()
+
+        @pl.when(jnp.logical_not(far_via))
+        def _():
+            copy_edge_s(side1, device1).start()
+
+    @pl.when(serves)
+    def _():
+        for c in range(CHUNKS):
+            to_via_q(c).wait_recv()
+            onward_q(c).start()
 
     for side, there, device in sides:
         @pl.when(there)
@@ -442,8 +631,36 @@
         )
         out[:, at] = jnp.where(inner, o / own_l[head], 0.0).astype(BF16)
 
+    for t, (there, device) in enumerate(corners):
+        @pl.when(there)
+        def _():
+            copy_corner_o(CORNERS - 1 - t, device).wait_recv()
+            copy_corner_s(CORNERS - 1 - t, device).wait_recv()
+
+    slot = iota((EDGE, DIM), 0) // RADIUS
+    real = real_slot(slot)
+    for side in range(2):
+        for lr in range(2):
+            t = 2 * side + lr
+            part = pl.ds(side * EDGE + lr * (EDGE - CORNER), CORNER)
+            first = 32 * (CORNERS - 1 - t)
+            stat = corner_s[t]
+            for head in range(HEADS):
+                m1 = stat[:, first + head : first + head + 1]
+                l1 = stat[:, first + HEADS + head : first + HEADS + head + 1]
+                o1 = corner_o[t * CORNER : (t + 1) * CORNER, lanes(head)]
+                top, total, mixed = merge(
+                    (edge_own_m[head, part], edge_own_l[head, part], edge_own_o[head, part]),
+                    (m1, l1, o1),
+                )
+                edge_own_m[head, part] = top
+                edge_own_l[head, part] = total
+                edge_own_o[head, part] = mixed
+
     for turn in range(2):
         side, there, device = edge_of(turn)
+        part = pl.ds(pl.multiple_of(side * EDGE, EDGE), EDGE)
+        place = jnp.where(side == 0, spread[:, 0:EDGE], spread[:, EDGE : 2 * EDGE])
 
         @pl.when(there)
         def _():
@@ -451,11 +668,7 @@
                 copy_edge_o(1 - side, c, device).wait_recv()
             copy_edge_s(1 - side, device).wait_recv()
 
-        part = pl.ds(pl.multiple_of(side * EDGE, EDGE), EDGE)
         stat = edge_s[side]
-        slot = iota((EDGE, DIM), 0) // RADIUS
-        real = (slot < COLS - RADIUS) | (slot >= SLOTS - RADIUS)
-        place = jnp.where(side == 0, spread[:, 0:EDGE], spread[:, EDGE : 2 * EDGE])
         for head in range(HEADS):
             at = lanes(head)
             top, total, mixed = merge(
@@ -463,24 +676,50 @@
                 (column(stat, head), column(stat, HEADS + head), edge_o[side, :, at]),
             )
             done = jnp.where(real, mixed / total, 0.0).astype(BF16)
-            out[:, at] = (out[:, at].astype(F32) + dot_nn(place, done)).astype(BF16)
+            out[:, at] = out[:, at] + dot_nn(place, done).astype(BF16)
+
+    @pl.when(serves)
+    def _():
+        for c in range(CHUNKS):
+            to_via_o(c).wait_recv()
+            onward_o(c).start()
+        to_via_s().wait_recv()
+        onward_s().start()
+        for c in range(CHUNKS):
+            onward_q(c).wait_send()
+            onward_o(c).wait_send()
+        onward_s().wait_send()
+
+    @pl.when(far_via)
+    def _():
+        for c in range(CHUNKS):
+            to_via_q(c).wait_send()
+            to_via_o(c).wait_send()
+        to_via_s().wait_send()
+
+    @pl.when(far_direct)
+    def _():
+        for c in range(CHUNKS):
+            far_q(c).wait_send()
+            copy_edge_o(side1, c, device1).wait_send()
+        copy_edge_s(side1, device1).wait_send()
 
     for c in range(CHUNKS):
-        @pl.when(has_down)
+        @pl.when(near_down)
         def _():
             copy_q_edge(0, c, down).wait_send()
             copy_edge_o(1, c, down).wait_send()
 
-        @pl.when(has_up)
+        @pl.when(near_up)
         def _():
             copy_q_edge(1, c, up).wait_send()
             copy_edge_o(0, c, up).wait_send()
 
-    @pl.when(has_down)
+    @pl.when(near_down)
     def _():
         copy_edge_s(1, down).wait_send()
 
-    @pl.when(has_up)
+    @pl.when(near_up)
     def _():
         copy_edge_s(0, up).wait_send()
 
@@ -488,10 +727,19 @@
         @pl.when(there)
         def _():
             copy_q_flank(side, device).wait_send()
-            for s in range(2):
-                copy_ext(side, s, device).wait_send()
             copy_flank_o(1 - side, device).wait_send()
             copy_flank_s(1 - side, device).wait_send()
+
+        @pl.when(there & far)
+        def _():
+            copy_ext(side, device).wait_send()
+
+    for t, (there, device) in enumerate(corners):
+        @pl.when(there)
+        def _():
+            copy_q_corner(t, device).wait_send()
+            copy_corner_o(t, device).wait_send()
+            copy_corner_s(t, device).wait_send()
 
 
 def on_device(nh, nw, queries, kv_new, kv_past):
@@ -513,35 +761,47 @@
             pltpu.VMEM((2 * FRAMES, 2 * EDGE, wide), BF16),
             pltpu.VMEM((2, EDGE, wide), BF16),
             pltpu.VMEM((2, FLANK, wide), BF16),
-            pltpu.VMEM((2, 2 * FRAMES, 2 * CORNER, wide), BF16),
+            pltpu.VMEM((CORNERS * CORNER, wide), BF16),
+            pltpu.VMEM((2 * FRAMES, 2 * CORNER, wide), BF16),
             pltpu.VMEM((HEADS, TOKENS, DIM), F32),
             pltpu.VMEM((HEADS, TOKENS, DIM), F32),
             pltpu.VMEM((HEADS, TOKENS, DIM), F32),
             pltpu.VMEM((HEADS, 2 * EDGE, DIM), F32),
             pltpu.VMEM((HEADS, 2 * EDGE, DIM), F32),
             pltpu.VMEM((HEADS, 2 * EDGE, DIM), F32),
-            pltpu.VMEM((4, EDGE, wide), BF16),
-            pltpu.VMEM((4, GROUP, DIM), F32),
+            pltpu.VMEM((5, EDGE, wide), BF16),
+            pltpu.VMEM((5, GROUP, DIM), F32),
             pltpu.VMEM((2, EDGE, wide), BF16),
             pltpu.VMEM((2, GROUP, DIM), F32),
             pltpu.VMEM((2, FLANK, wide), BF16),
             pltpu.VMEM((2, GROUP, DIM), F32),
+            pltpu.VMEM((CORNERS * CORNER, wide), BF16),
+            pltpu.VMEM((CORNERS, GROUP, DIM), F32),
+            pltpu.VMEM((EDGE, wide), BF16),
+            pltpu.VMEM((EDGE, wide), BF16),
+            pltpu.VMEM((GROUP, DIM), F32),
             pltpu.VMEM((REACH0, CUT), F32),
             pltpu.VMEM((TOKENS - REACH1, CUT), F32),
             pltpu.VMEM((2, FLANK, (FRAMES + 1) * FLANK), F32),
-            pltpu.VMEM((2, EDGE, FRAMES * SPAN), F32),
+            pltpu.VMEM((2, EDGE, (FRAMES + 1) * EDGE), F32),
+            pltpu.VMEM((EDGE, FRAMES * SPAN), F32),
+            pltpu.VMEM((EDGE, (FRAMES + 1) * EDGE), F32),
             pltpu.VMEM((2 * EDGE, TOKENS), BF16),
             pltpu.VMEM((TOKENS, 2 * EDGE), BF16),
             dma((1 + 2 * FRAMES,)),
             dma((2, 2, CHUNKS)),
             dma((2, 2)),
-            dma((2, 2, 2)),
+            dma((2, CORNERS)),
+            dma((2, 2)),
             dma((2, 2, CHUNKS)),
             dma((2, 2)),
-            dma((2, 4)),
+            dma((2, CORNERS)),
+            dma((2, 8)),
+            dma((2, 2 * CHUNKS + 1)),
+            dma((2 * CHUNKS + 1,)),
         ],
         compiler_params=pltpu.CompilerParams(
-            collective_id=0, has_side_effects=True, vmem_limit_bytes=60 * 1024 * 1024
+            collective_id=0, has_side_effects=True, vmem_limit_bytes=VMEM_BYTES
         ),
     )(queries, kv_new, kv_past)
     return out.reshape(COLS, ROWS, wide).transpose(1, 0, 2)

time: 46.3 us -> 40.2 us (0.87)
  Pallas kernels: 44.3 us -> 39.3 us
  local copies, waits for them, and re-layouts: 1.82 us -> 0.77 us
    pallas_call x1, Pallas kernels: 44.3 us -> 39.3 us  [on_device(): pl.pallas_call(functools.partial(kernel, nh, nw), out_shape=jax.ShapeDtyp...]
    unnamed x1, local copies, waits for them, and re-layouts: 1.82 us -> 0.77 us
where the time goes in v3:
time: 40.2 us; the launch traced here: 40.1 us
  Pallas kernels  39.3 us (98%)
  local copies, waits for them, and re-layouts  0.77 us (2%)
    pallas_call x1, Pallas kernels, on_device(): pl.pallas_call(functools.partial(kernel, nh, nw), out_shape=jax.ShapeDtyp...  39.3 us

profile of v3, /device:TPU:31, one launch (start us, length us, event | category | flops | bytes accessed | tf_op | source)
XLA Modules:
  0.0 40.1 jit_solution(1473342177232515135)
XLA Ops:
  0.0 39.3 %shard_map.37 = bf16[224,1024]{1,0:T(8,128)(2,1)S(1)} custom-call(bf16[224,1024]{1,0:T(8,128)(2,1)} %bitcast.15, bf16[2,224,1024]{2,1,0:T(8,128)(2,1)} %bitcast.14, bf16[2,2,224,1024]{3,2,1,0:T(8,128)(2,1)} %bitcast.13), custom_call_target="tpu_custom_call" | custom-call | tf_op jit(solution)/shard_map/pallas_call | solution.py:752
  39.3 0.8 %copy.5 = bf16[16,14,1024]{2,0,1:T(8,128)(2,1)} copy(bf16[16,14,1024]{2,0,1:T(8,128)(2,1)S(1)} %bitcast.12) | data formatting | bytes 917504

commit v4 on v3

--- a/solution.py
+++ b/solution.py
@@ -33,7 +33,7 @@
 BLOCK1 = TOKENS - CUT
 REACH0 = 12 * ROWS
 REACH1 = 4 * ROWS
-OWN_UNROLL = 8
+OWN_UNROLL = 2
 
 
 def dot_nt(a, b):
@@ -114,6 +114,7 @@
     other_via = (jnp.where(far_down, via_up, via_down), w)
     far_via, far_direct = far & relayed, far & jnp.logical_not(relayed)
     across = (nh // 2 - flip, w)
+    patient = far_down & far_direct & (w // 4 == nw // 8 - 1)
     greet = near + ((far_via, other_via), (far_direct, across), (serves, served))
     awaited = [there for there, _ in near] + [far, serves]
 
@@ -315,7 +316,7 @@
         def _():
             to_via_q(c).start()
 
-        @pl.when(far_direct)
+        @pl.when(far_direct & jnp.logical_not(patient))
         def _():
             far_q(c).start()
 
@@ -326,6 +327,11 @@
         @pl.when(near_up)
         def _():
             copy_q_edge(1, c, up).start()
+
+    @pl.when(patient)
+    def _():
+        for c in range(CHUNKS):
+            far_q(c).start()
 
     @pl.when(has_right)
     def _():

time: 40.2 us -> 40.6 us (level)
  the two profiles are of different devices: /device:TPU:31 before, /device:TPU:39 now
where the time goes in v4:
time: 40.6 us; the launch traced here: 40.5 us
  Pallas kernels  39.7 us (98%)
  local copies, waits for them, and re-layouts  0.77 us (2%)
    pallas_call x1, Pallas kernels, on_device(): pl.pallas_call(functools.partial(kernel, nh, nw), out_shape=jax.ShapeDtyp...  39.7 us

profile of v4, /device:TPU:39, one launch (start us, length us, event | category | flops | bytes accessed | tf_op | source)
XLA Modules:
  0.0 40.5 jit_solution(15907224205207295535)
XLA Ops:
  0.0 39.7 %shard_map.37 = bf16[224,1024]{1,0:T(8,128)(2,1)S(1)} custom-call(bf16[224,1024]{1,0:T(8,128)(2,1)} %bitcast.15, bf16[2,224,1024]{2,1,0:T(8,128)(2,1)} %bitcast.14, bf16[2,2,224,1024]{3,2,1,0:T(8,128)(2,1)} %bitcast.13), custom_call_target="tpu_custom_call" | custom-call | tf_op jit(solution)/shard_map/pallas_call | solution.py:758
  39.7 0.8 %copy.5 = bf16[16,14,1024]{2,0,1:T(8,128)(2,1)} copy(bf16[16,14,1024]{2,0,1:T(8,128)(2,1)S(1)} %bitcast.12) | data formatting | bytes 917504

commit v5 on v4

--- a/solution.py
+++ b/solution.py
@@ -33,7 +33,7 @@
 BLOCK1 = TOKENS - CUT
 REACH0 = 12 * ROWS
 REACH1 = 4 * ROWS
-OWN_UNROLL = 2
+OWN_UNROLL = 8
 
 
 def dot_nt(a, b):

time: 40.6 us -> 40.2 us (level)
  the two profiles are of different devices: /device:TPU:39 before, /device:TPU:31 now
where the time goes in v5:
time: 40.2 us; the launch traced here: 40.1 us
  Pallas kernels  39.3 us (98%)
  local copies, waits for them, and re-layouts  0.77 us (2%)
    pallas_call x1, Pallas kernels, on_device(): pl.pallas_call(functools.partial(kernel, nh, nw), out_shape=jax.ShapeDtyp...  39.3 us

profile of v5, /device:TPU:31, one launch (start us, length us, event | category | flops | bytes accessed | tf_op | source)
XLA Modules:
  0.0 40.1 jit_solution(8456010283538323300)
XLA Ops:
  0.0 39.3 %shard_map.37 = bf16[224,1024]{1,0:T(8,128)(2,1)S(1)} custom-call(bf16[224,1024]{1,0:T(8,128)(2,1)} %bitcast.15, bf16[2,224,1024]{2,1,0:T(8,128)(2,1)} %bitcast.14, bf16[2,2,224,1024]{3,2,1,0:T(8,128)(2,1)} %bitcast.13), custom_call_target="tpu_custom_call" | custom-call | tf_op jit(solution)/shard_map/pallas_call | solution.py:758
  39.3 0.8 %copy.5 = bf16[16,14,1024]{2,0,1:T(8,128)(2,1)} copy(bf16[16,14,1024]{2,0,1:T(8,128)(2,1)S(1)} %bitcast.12) | data formatting | bytes 917504
